TPU v7x, 512 devices: a whole 4x8x8 slice. The times are simulated.
512 devices in a mesh: ctx: 32 (over x, y), tp: 16 (over z, core).
Axes of the slice: x: 4, y: 8, z: 8, core: 2. Of those that a mesh axis runs over, the one named last changes fastest.
Arguments:
- gate_in: bfloat16 [16384, 4096], P('ctx', 'tp'), may hold values from -6 to 6
- key_in: bfloat16 [16384, 4096], P('ctx', 'tp'), may hold values from -6 to 6
- value_in: bfloat16 [16384, 4096], P('ctx', 'tp'), may hold values from -60 to 60
- filters: bfloat16 [16384, 4096], P('ctx', 'tp'), may hold values from -1 to 1
- skip: float32 [4096], P('tp'), may hold values from -1 to 1
- gain: float32 [4096], P('tp'), may hold values from 0.1 to 1.9
Outputs:
- output: bfloat16 [16384, 4096], P('ctx', 'tp')
All inputs are finite; a program needn't handle non-finite values.
Results may differ from a plain program's by a relative error of at most 0.0049.
Values may be sent and summed in bfloat16 or wider, within the bound.
No kernel may reach another device: no remote copies, remote signals or barrier semaphores. Data moves between devices by JAX's collectives and lax.ppermute only.
A program may use at most 64 MiB of HBM per device.

v0:
```python
import math

import jax
import jax.numpy as jnp
from jax import lax
from jax.sharding import PartitionSpec as P

HIGHEST_PREC = lax.Precision.HIGHEST
EPSILON = 1e-05
RADIX = 16
DIRECT_MAX = 256


def phase_table(row_count, col_count, period, sign):
    row_ids = jnp.arange(row_count, dtype=jnp.int32)[:, None]
    col_ids = jnp.arange(col_count, dtype=jnp.int32)[None, :]
    phase = (row_ids * col_ids % period).astype(jnp.float32) * (2.0 * math.pi / period)
    return (jnp.cos(phase), sign * jnp.sin(phase))


def complex_product(spec, cos_tab, sin_tab, real_part, imag_part):

    def contract(table, data):
        return jnp.einsum(spec, table, data, precision=HIGHEST_PREC)

    if imag_part is None:
        return (contract(cos_tab, real_part), contract(sin_tab, real_part))
    return (
        contract(cos_tab, real_part) - contract(sin_tab, imag_part),
        contract(cos_tab, imag_part) + contract(sin_tab, real_part),
    )


def forward_last(real_part, imag_part, length):
    live_rows = real_part.shape[-1]
    leading = real_part.shape[:-1]
    if length <= DIRECT_MAX:
        cos_tab, sin_tab = phase_table(live_rows, length, length, -1.0)
        return complex_product("tk,...t->...k", cos_tab, sin_tab, real_part, imag_part)
    inner = length // RADIX
    outer_live = live_rows // inner
    real_part = real_part.reshape(leading + (outer_live, inner))
    imag_part = imag_part.reshape(leading + (outer_live, inner))
    cos_tab, sin_tab = phase_table(outer_live, RADIX, RADIX, -1.0)
    real_part, imag_part = complex_product(
        "ak,...ab->...kb", cos_tab, sin_tab, real_part, imag_part
    )
    twist_cos, twist_sin = phase_table(RADIX, inner, length, -1.0)
    real_part, imag_part = (
        real_part * twist_cos - imag_part * twist_sin,
        real_part * twist_sin + imag_part * twist_cos,
    )
    real_part, imag_part = forward_last(real_part, imag_part, inner)
    return (real_part.reshape(leading + (length,)), imag_part.reshape(leading + (length,)))


def inverse_last(real_part, imag_part, length, keep_rows):
    leading = real_part.shape[:-1]
    if length <= DIRECT_MAX:
        cos_tab, sin_tab = phase_table(length, keep_rows, length, 1.0)
        return complex_product("kt,...k->...t", cos_tab, sin_tab, real_part, imag_part)
    inner = length // RADIX
    outer_keep = keep_rows // inner
    real_part = real_part.reshape(leading + (RADIX, inner))
    imag_part = imag_part.reshape(leading + (RADIX, inner))
    real_part, imag_part = inverse_last(real_part, imag_part, inner, inner)
    twist_cos, twist_sin = phase_table(RADIX, inner, length, 1.0)
    real_part, imag_part = (
        real_part * twist_cos - imag_part * twist_sin,
        real_part * twist_sin + imag_part * twist_cos,
    )
    cos_tab, sin_tab = phase_table(RADIX, outer_keep, RADIX, 1.0)
    real_part, imag_part = complex_product(
        "kt,...kb->...tb", cos_tab, sin_tab, real_part, imag_part
    )
    return (
        real_part.reshape(leading + (outer_keep * inner,)),
        imag_part.reshape(leading + (outer_keep * inner,)),
    )


def spectral_product(spec_re, spec_im):
    prod_re = spec_re[0] * spec_re[1] - spec_im[0] * spec_im[1]
    prod_im = spec_re[0] * spec_im[1] + spec_im[0] * spec_re[1]
    return (prod_re, prod_im)


def sequence_conv(mixed, filters, ctx_size, total_len):
    tok_rows, channels = mixed.shape
    block_rows = tok_rows // ctx_size
    ctx_index = lax.axis_index("ctx")
    pieces = (
        lax.all_to_all(
            mixed.reshape(ctx_size, block_rows, channels),
            "ctx",
            split_axis=0,
            concat_axis=0,
            tiled=True,
        ),
        lax.all_to_all(
            filters.reshape(ctx_size, block_rows, channels),
            "ctx",
            split_axis=0,
            concat_axis=0,
            tiled=True,
        ),
    )
    stacked = jnp.stack(pieces).astype(jnp.float32)
    cos_tab, sin_tab = phase_table(2 * ctx_size, ctx_size, 2 * ctx_size, -1.0)
    part_re, part_im = complex_product("kq,sqmc->skmc", cos_tab, sin_tab, stacked, None)
    positions = ctx_index * block_rows + jnp.arange(block_rows, dtype=jnp.int32)
    freq_ids = jnp.arange(2 * ctx_size, dtype=jnp.int32)
    phase = (freq_ids[:, None] * positions[None, :] % total_len).astype(jnp.float32) * (
        2.0 * math.pi / total_len
    )
    twist_cos = jnp.cos(phase)[None, :, :, None]
    twist_sin = -jnp.sin(phase)[None, :, :, None]
    part_re, part_im = (
        part_re * twist_cos - part_im * twist_sin,
        part_re * twist_sin + part_im * twist_cos,
    )
    part_re, part_im = (
        lax.all_to_all(part_re, "ctx", split_axis=1, concat_axis=2, tiled=True),
        lax.all_to_all(part_im, "ctx", split_axis=1, concat_axis=2, tiled=True),
    )
    part_re = part_re.transpose(0, 1, 3, 2)
    part_im = part_im.transpose(0, 1, 3, 2)
    spec_re, spec_im = forward_last(part_re, part_im, tok_rows)
    prod_re, prod_im = spectral_product(spec_re, spec_im)
    back_re, back_im = inverse_last(prod_re, prod_im, tok_rows, tok_rows)
    own_freq = 2 * ctx_index + jnp.arange(2, dtype=jnp.int32)
    local_pos = jnp.arange(tok_rows, dtype=jnp.int32)
    phase = (own_freq[:, None] * local_pos[None, :] % total_len).astype(jnp.float32) * (
        2.0 * math.pi / total_len
    )
    twist_cos = jnp.cos(phase)[:, None, :]
    twist_sin = jnp.sin(phase)[:, None, :]
    back_re, back_im = (
        back_re * twist_cos - back_im * twist_sin,
        back_re * twist_sin + back_im * twist_cos,
    )
    back_re = back_re.transpose(0, 2, 1)
    back_im = back_im.transpose(0, 2, 1)
    back_re, back_im = (
        lax.all_to_all(back_re, "ctx", split_axis=1, concat_axis=0, tiled=True),
        lax.all_to_all(back_im, "ctx", split_axis=1, concat_axis=0, tiled=True),
    )
    cos_tab, sin_tab = phase_table(ctx_size, 2 * ctx_size, 2 * ctx_size, 1.0)
    conv = (
        jnp.einsum("qk,kmc->qmc", cos_tab, back_re, precision=HIGHEST_PREC)
        - jnp.einsum("qk,kmc->qmc", sin_tab, back_im, precision=HIGHEST_PREC)
    ) / total_len
    conv = lax.all_to_all(conv, "ctx", split_axis=0, concat_axis=0, tiled=True)
    return conv.reshape(tok_rows, channels)


def per_device(gate_in, key_in, value_in, filters, skip, gain):
    tok_rows, channels = key_in.shape
    mixed = (key_in.astype(jnp.float32) * value_in.astype(jnp.float32)).astype(jnp.bfloat16)
    ctx_size = lax.axis_size("ctx")
    total_len = 2 * tok_rows * ctx_size
    conv = sequence_conv(mixed, filters, ctx_size, total_len)
    summed = conv + skip[None, :] * mixed.astype(jnp.float32)
    energy = lax.psum(jnp.sum(summed * summed, axis=1), "tp")
    scale_row = lax.rsqrt(energy / (channels * lax.axis_size("tp")) + EPSILON)
    return (gate_in.astype(jnp.float32) * summed * scale_row[:, None] * gain[None, :]).astype(
        jnp.bfloat16
    )


def solution(mesh):
    in_specs = (P("ctx", "tp"), P("ctx", "tp"), P("ctx", "tp"), P("ctx", "tp"), P("tp"), P("tp"))
    out_specs = P("ctx", "tp")
    return jax.shard_map(
        per_device, mesh=mesh, in_specs=in_specs, out_specs=out_specs, check_vma=False
    )
```

profile of v0, /device:TPU:1, one launch (start us, length us, event | category | flops | bytes accessed | tf_op | source)
XLA Modules:
  0.0 308.6 jit_solution(1107300280049825855)
XLA Ops:
  1.1 20.0 %all_to_all.87 = bf16[32,16,256]{2,1,0:T(8,128)(2,1)S(1)} all-to-all(bf16[32,16,256]{2,1,0:T(8,128)(2,1)S(1)} %bitcast.185), channel_id=1, replica_groups=mesh['ctx'=32,'tp'=16] {'ctx'}, dimensions={0} | all-to-all | bytes 524288 | tf_op jit(solution)/shard_map/all_to_all | solution.py:93
  21.1 6.3 %all-to-all-start.1 = ((bf16[32,16,256]{2,1,0:T(8,128)(2,1)}), bf16[32,16,256]{2,1,0:T(8,128)(2,1)S(1)}, u32[]{:S(2)}, u32[]{:S(2)}) async-start(bf16[32,16,256]{2,1,0:T(8,128)(2,1)} %bitcast.194), calls=%async_computation.1 | async-start | bytes 524288 | tf_op jit(solution)/shard_map/all_to_all | solution.py:100
  27.6 9.4 %all-to-all-done.1 = bf16[32,16,256]{2,1,0:T(8,128)(2,1)S(1)} async-done(((bf16[32,16,256]{2,1,0:T(8,128)(2,1)}), bf16[32,16,256]{2,1,0:T(8,128)(2,1)S(1)}, u32[]{:S(2)}, u32[]{:S(2)}) %all-to-all-start.1) | async-done | bytes 262176 | tf_op jit(solution)/shard_map/all_to_all | solution.py:100
  38.2 3.0 fusion.2
  41.2 2.6 copy.104
  43.8 5.7 %all-to-all-start.3 = ((f32[2,64,16,256]{3,2,0,1:T(8,128)}), f32[2,64,16,256]{3,2,0,1:T(8,128)S(1)}, u32[]{:S(2)}, u32[]{:S(2)}) async-start(f32[2,64,16,256]{3,2,0,1:T(8,128)} %copy.104), calls=%async_computation.3 | async-start | bytes 4194304 | tf_op jit(solution)/shard_map/all_to_all | solution.py:124
  49.5 4.1 %copy.100 = f32[2,64,16,256]{3,2,0,1:T(8,128)} copy(f32[2,64,16,256]{3,1,2,0:T(8,128)} %get-tuple-element.7) | data formatting | bytes 4194304 | tf_op jit(solution)/shard_map/sub | solution.py:119
  53.7 44.8 %all-to-all-done.3 = f32[2,64,16,256]{3,2,0,1:T(8,128)S(1)} async-done(((f32[2,64,16,256]{3,2,0,1:T(8,128)}), f32[2,64,16,256]{3,2,0,1:T(8,128)S(1)}, u32[]{:S(2)}, u32[]{:S(2)}) %all-to-all-start.3) | async-done | bytes 2097184 | tf_op jit(solution)/shard_map/all_to_all | solution.py:124
  98.5 5.4 %all-to-all-start.2 = ((f32[2,64,16,256]{3,2,0,1:T(8,128)}), f32[2,64,16,256]{3,2,0,1:T(8,128)}, u32[]{:S(2)}, u32[]{:S(2)}) async-start(f32[2,64,16,256]{3,2,0,1:T(8,128)} %copy.100), calls=%async_computation.2 | async-start | bytes 4194304 | tf_op jit(solution)/shard_map/all_to_all | solution.py:123
  104.6 4.4 %fusion.14 = f32[2,2,256,32,16]{2,4,3,1,0:T(8,128)} fusion(f32[2,2,256,16,32]{2,4,3,1,0:T(8,128)S(1)} %bitcast.182), kind=kOutput, calls=%fused_computation.22 | convolution fusion | flops 100667136 | bytes 4194304 | tf_op jit(solution)/shard_map/ak,...ab->...kb/dot_general | solution.py:24
  109.0 3.1 %fusion.12 = f32[2,2,256,32,16]{2,4,3,1,0:T(8,128)S(1)} fusion(f32[2,2,256,16,32]{2,4,3,1,0:T(8,128)S(1)} %bitcast.183), kind=kOutput, calls=%fused_computation.20 | convolution fusion | flops 100666880 | bytes 4194304 | tf_op jit(solution)/shard_map/ak,...ab->...kb/dot_general | solution.py:24
  112.1 39.8 %all-to-all-done.2 = f32[2,64,16,256]{3,2,0,1:T(8,128)} async-done(((f32[2,64,16,256]{3,2,0,1:T(8,128)}), f32[2,64,16,256]{3,2,0,1:T(8,128)}, u32[]{:S(2)}, u32[]{:S(2)}) %all-to-all-start.2) | async-done | bytes 2097184 | tf_op jit(solution)/shard_map/all_to_all | solution.py:123
  154.2 3.3 %fusion.20 = f32[2,2,256,32,16]{2,4,3,1,0:T(8,128)S(1)} fusion(f32[2,2,256,32,16]{2,4,3,1,0:T(8,128)S(1)} %copy-done, f32[2,2,256,16,32]{2,4,3,1,0:T(8,128)S(1)} %bitcast.180), kind=kOutput, calls=%fused_computation.28 | convolution fusion | flops 101191168 | bytes 6291456 | tf_op jit(solution)/shard_map/ak,...ab->...kb/dot_general | solution.py:24
  157.5 3.9 %fusion = (f32[2,2,256,16,32]{2,3,4,1,0:T(8,128)S(1)}, f32[2,2,256,16,32]{2,3,4,1,0:T(8,128)S(1)}) fusion(f32[2,2,256,32,16]{2,4,3,1,0:T(8,128)S(1)} %fusion.20, f32[16,32]{0,1:T(8,128)S(1)} %copy.111, f32[16,32]{0,1:T(8,128)S(1)} %copy.108, f32[2,2,256,32,16]{2,4,3,1,0:T(8,128)S(1)} %fusion.12, f32[2,2,256,16,32]{2,4,3,1,0:T(8,128)S(1)} %bitcast.181), kind=kOutput, calls=%fused_computation.2 | convolution fusion | flops 104337152 | bytes 10489856 | tf_op jit(solution)/shard_map/ak,...ab->...kb/dot_general | solution.py:24
  161.4 3.3 %fusion.6 = f32[2,2,256,16,32]{2,4,3,1,0:T(8,128)S(1)} fusion(f32[2,2,256,16,32]{2,3,4,1,0:T(8,128)S(1)} %get-tuple-element.6), kind=kOutput, calls=%fused_computation.14 | convolution fusion | flops 201341952 | bytes 4194304 | tf_op jit(solution)/shard_map/tk,...t->...k/dot_general | solution.py:24
  164.7 3.2 %fusion.4 = f32[2,2,256,16,32]{2,4,3,1,0:T(8,128)S(1)} fusion(f32[2,2,256,16,32]{2,3,4,1,0:T(8,128)S(1)} %get-tuple-element.6), kind=kOutput, calls=%fused_computation.12 | convolution fusion | flops 201340928 | bytes 4194304 | tf_op jit(solution)/shard_map/tk,...t->...k/dot_general | solution.py:24
  168.0 3.4 %fusion.26 = f32[2,2,256,16,32]{2,4,3,1,0:T(8,128)S(1)} fusion(f32[2,2,256,16,32]{2,4,3,1,0:T(8,128)S(1)} %fusion.6, f32[2,2,256,16,32]{2,3,4,1,0:T(8,128)S(1)} %get-tuple-element.5), kind=kOutput, calls=%fused_computation.30 | convolution fusion | flops 201865216 | bytes 6291456 | tf_op jit(solution)/shard_map/tk,...t->...k/dot_general | solution.py:24
  171.4 3.8 %fusion.29 = f32[2,2,256,16,32]{2,4,3,1,0:T(8,128)S(1)} fusion(f32[2,2,256,16,32]{2,4,3,1,0:T(8,128)S(1)} %fusion.4, f32[2,2,256,16,32]{2,3,4,1,0:T(8,128)S(1)} %get-tuple-element.5), kind=kOutput, calls=%fused_computation.31 | convolution fusion | flops 201866240 | bytes 6291456 | tf_op jit(solution)/shard_map/tk,...t->...k/dot_general | solution.py:24
  190.5 5.9 %all-to-all-start.4 = ((f32[2,512,256]{2,0,1:T(2,128)}), f32[2,512,256]{2,0,1:T(2,128)S(1)}, u32[]{:S(2)}, u32[]{:S(2)}) async-start(f32[2,512,256]{2,0,1:T(2,128)} %copy.122), calls=%async_computation.4 | async-start | bytes 2097152 | tf_op jit(solution)/shard_map/all_to_all | solution.py:145
  198.2 21.3 %all-to-all-done.4 = f32[2,512,256]{2,0,1:T(2,128)S(1)} async-done(((f32[2,512,256]{2,0,1:T(2,128)}), f32[2,512,256]{2,0,1:T(2,128)S(1)}, u32[]{:S(2)}, u32[]{:S(2)}) %all-to-all-start.4) | async-done | bytes 1048608 | tf_op jit(solution)/shard_map/all_to_all | solution.py:145
  219.5 7.8 %all-to-all-start.5 = ((f32[2,512,256]{2,0,1:T(2,128)}), f32[2,512,256]{2,0,1:T(2,128)S(1)}, u32[]{:S(2)}, u32[]{:S(2)}) async-start(f32[2,512,256]{2,0,1:T(2,128)} %copy.125), calls=%async_computation.5 | async-start | bytes 2097152 | tf_op jit(solution)/shard_map/all_to_all | solution.py:146
  230.4 18.3 %all-to-all-done.5 = f32[2,512,256]{2,0,1:T(2,128)S(1)} async-done(((f32[2,512,256]{2,0,1:T(2,128)}), f32[2,512,256]{2,0,1:T(2,128)S(1)}, u32[]{:S(2)}, u32[]{:S(2)}) %all-to-all-start.5) | async-done | bytes 1048608 | tf_op jit(solution)/shard_map/all_to_all | solution.py:146
  251.4 19.9 %all_to_all.88 = f32[32,16,256]{2,1,0:T(8,128)S(1)} all-to-all(f32[32,16,256]{2,1,0:T(8,128)S(1)} %copy.128), channel_id=1, replica_groups=mesh['ctx'=32,'tp'=16] {'ctx'}, dimensions={0} | all-to-all | bytes 1048576 | tf_op jit(solution)/shard_map/all_to_all | solution.py:153
  271.5 36.1 %psum.7 = f32[512]{0:T(512)S(1)} all-reduce(f32[512]{0:T(512)S(1)} %multiply_reduce_fusion), channel_id=1, replica_groups=mesh['ctx'=32,'tp'=16] {'tp'}, use_global_device_ids=true, to_apply=%region_1.2 | all-reduce | flops 512 | bytes 4096 | tf_op jit(solution)/shard_map/psum | solution.py:164
  (51 shorter events, 29.2 us)
Async XLA Ops:
  21.1 16.0 %all-to-all-start.1 = ((bf16[32,16,256]{2,1,0:T(8,128)(2,1)}), bf16[32,16,256]{2,1,0:T(8,128)(2,1)S(1)}, u32[]{:S(2)}, u32[]{:S(2)}) async-start(bf16[32,16,256]{2,1,0:T(8,128)(2,1)} %bitcast.194), calls=%async_computation.1 | async-start | bytes 524288 | tf_op jit(solution)/shard_map/all_to_all | solution.py:100
  43.8 54.7 %all-to-all-start.3 = ((f32[2,64,16,256]{3,2,0,1:T(8,128)}), f32[2,64,16,256]{3,2,0,1:T(8,128)S(1)}, u32[]{:S(2)}, u32[]{:S(2)}) async-start(f32[2,64,16,256]{3,2,0,1:T(8,128)} %copy.104), calls=%async_computation.3 | async-start | bytes 4194304 | tf_op jit(solution)/shard_map/all_to_all | solution.py:124
  98.5 53.5 %all-to-all-start.2 = ((f32[2,64,16,256]{3,2,0,1:T(8,128)}), f32[2,64,16,256]{3,2,0,1:T(8,128)}, u32[]{:S(2)}, u32[]{:S(2)}) async-start(f32[2,64,16,256]{3,2,0,1:T(8,128)} %copy.100), calls=%async_computation.2 | async-start | bytes 4194304 | tf_op jit(solution)/shard_map/all_to_all | solution.py:123
  151.9 2.2 copy-start
  190.5 29.0 %all-to-all-start.4 = ((f32[2,512,256]{2,0,1:T(2,128)}), f32[2,512,256]{2,0,1:T(2,128)S(1)}, u32[]{:S(2)}, u32[]{:S(2)}) async-start(f32[2,512,256]{2,0,1:T(2,128)} %copy.122), calls=%async_computation.4 | async-start | bytes 2097152 | tf_op jit(solution)/shard_map/all_to_all | solution.py:145
  219.5 29.2 %all-to-all-start.5 = ((f32[2,512,256]{2,0,1:T(2,128)}), f32[2,512,256]{2,0,1:T(2,128)S(1)}, u32[]{:S(2)}, u32[]{:S(2)}) async-start(f32[2,512,256]{2,0,1:T(2,128)} %copy.125), calls=%async_computation.5 | async-start | bytes 2097152 | tf_op jit(solution)/shard_map/all_to_all | solution.py:146
  248.8 1.6 copy-start.1
  250.4 21.0 %copy-start.3 = (f32[256]{0:T(256)S(1)}, f32[256]{0:T(256)}, u32[]{:S(2)}) copy-start(f32[256]{0:T(256)} %param.10) | copy-start | bytes 3076
  250.4 57.2 %copy-start.2 = (bf16[512,256]{1,0:T(8,128)(2,1)S(1)}, bf16[512,256]{1,0:T(8,128)(2,1)}, u32[]{:S(2)}) copy-start(bf16[512,256]{1,0:T(8,128)(2,1)} %param.6) | copy-start | bytes 786436
  250.4 57.2 %copy-start.4 = (f32[256]{0:T(256)S(1)}, f32[256]{0:T(256)}, u32[]{:S(2)}) copy-start(f32[256]{0:T(256)} %param.11) | copy-start | bytes 3076
where the time goes:
time: 315 us; the launch traced here: 309 us
  waiting for transfers between devices  134 us (43%)
  blocking collectives  76 us (24%)
  matrix products  46.2 us (15%)
  starting transfers between devices  31.1 us (10%)
  local copies, waits for them, and re-layouts  17.8 us (6%)
  other arithmetic  3.36 us (1%)
    all_to_all x1, waiting for transfers between devices, sequence_conv(): lax.all_to_all(part_im, 'ctx', split_axis=1, concat_axis=2, tiled=True)  44.8 us
    dot_general x18, matrix products, contract(): return jnp.einsum(spec, table, data, precision=HIGHEST_PREC)  44 us
    all_to_all x1, waiting for transfers between devices, sequence_conv(): lax.all_to_all(part_re, 'ctx', split_axis=1, concat_axis=2, tiled=True)  39.8 us
    psum x1, blocking collectives, per_device(): energy = lax.psum(jnp.sum(summed * summed, axis=1), 'tp')  36.1 us
    all_to_all x1, waiting for transfers between devices, sequence_conv(): lax.all_to_all(back_re, 'ctx', split_axis=1, concat_axis=0, tiled=True)  21.3 us
    all_to_all x1, blocking collectives, sequence_conv(): lax.all_to_all(mixed.reshape(ctx_size, block_rows, channels), 'ctx', spli...  20 us
    all_to_all x1, blocking collectives, sequence_conv(): conv = lax.all_to_all(conv, 'ctx', split_axis=0, concat_axis=0, tiled=True)  19.9 us
    all_to_all x1, waiting for transfers between devices, sequence_conv(): lax.all_to_all(back_im, 'ctx', split_axis=1, concat_axis=0, tiled=True)  18.3 us
  transfers between devices with their start and end apart: 5, of which 5 were waited for; matrix products, arithmetic and copies ran while one was open for 5% of the time, Pallas kernels for 0%

commit v1 on v0

v1 whole, which is shorter than its diff:
```python
import functools

import jax
import jax.numpy as jnp
from jax import lax
from jax.experimental import pallas as pl
from jax.experimental.pallas import tpu as pltpu
from jax.sharding import PartitionSpec as P

EPSILON = 1e-05
LANES = 128
GROUP = 8
PAD = 16
F32 = jnp.float32
BF16 = jnp.bfloat16


def whole(shape=None):
    return pl.BlockSpec(memory_space=pltpu.VMEM)


def flip_blocks(rows):
    parts = []
    for a in range(rows.shape[0] // LANES):
        block = rows[a * LANES : (a + 1) * LANES, :].T
        parts.append(block.reshape(block.shape[0] // GROUP, GROUP, LANES))
    return jnp.concatenate(parts, axis=1)


def pack_kernel(key_ref, value_ref, taps_ref, out_ref):
    mixed = key_ref[...].astype(F32) * value_ref[...].astype(F32)
    half = out_ref.shape[1] // 2
    out_ref[:, :half, :] = flip_blocks(mixed).astype(BF16)
    out_ref[:, half:, :] = flip_blocks(taps_ref[...].astype(F32)).astype(BF16)


def conv_kernel(recv_ref, skip_ref, out_ref, x_all, h_all, y_all, x_pad, h_pad, odd_pad, acc, toe_a, toe_b):
    owners, both, _ = recv_ref.shape
    half = both // 2
    x_all[...] = recv_ref[:, :half, :].astype(F32).reshape(owners * half, LANES)
    h_all[...] = recv_ref[:, half:, :].astype(F32).reshape(owners * half, LANES)
    x_pad[:PAD, :] = jnp.zeros((PAD, LANES), F32)
    h_pad[:8, :] = jnp.zeros((8, LANES), F32)
    odd_pad[:8, :] = jnp.zeros((8, LANES), F32)
    lane = lax.broadcasted_iota(jnp.int32, (8, LANES), 1)
    row = lax.broadcasted_iota(jnp.int32, (8, LANES), 0)
    edge = lane + row

    def toeplitz(k):
        now = jnp.broadcast_to(h_pad[8 + k : 9 + k, :], (8, LANES))
        before = jnp.broadcast_to(h_pad[7 + k : 8 + k, :], (8, LANES))
        tiles = []
        for v in range(LANES // 8):
            mixed_row = jnp.where(edge >= LANES - 8 * v, before, now)
            tiles.append(pltpu.roll(mixed_row, 8 * v, 1, stride=1, stride_axis=0))
        return jnp.concatenate(tiles, axis=0).astype(BF16)

    def channel(c, carry):
        x = x_all[pl.ds(c, LANES, stride=GROUP), :]
        x_pad[PAD:, :] = x
        h_pad[8:, :] = h_all[pl.ds(c, LANES, stride=GROUP), :]
        lhs = jnp.concatenate(
            [x_pad[PAD - b : PAD - b + LANES, :].astype(BF16) for b in range(0, 16, 2)], axis=1
        )
        for a in range(8):
            toe = (toe_a, toe_b)[a % 2]
            for b in range(0, 16, 2):
                for e in range(2):
                    toe[b // 2 * LANES : (b // 2 + 1) * LANES, e * LANES : (e + 1) * LANES] = toeplitz(
                        16 * a + b + e
                    )
            part = jnp.dot(lhs[: LANES - 16 * a, :], toe[...], preferred_element_type=F32)
            if a == 0:
                acc[...] = part
            else:
                acc[16 * a :, :] += part
        odd_pad[8:, :] = acc[:, LANES:]
        conv = acc[:, :LANES] + odd_pad[7 : 7 + LANES, :]
        y_all[pl.ds(c, LANES, stride=GROUP), :] = conv + skip_ref[c] * x
        return carry

    lax.fori_loop(0, GROUP, channel, 0)
    out_ref[...] = y_all[...].reshape(out_ref.shape).astype(BF16)


def energy_kernel(back_ref, out_ref):
    owners, rows, _ = back_ref.shape
    values = back_ref[...].astype(F32).reshape(owners, rows // GROUP, GROUP, LANES)
    total = jnp.sum(values * values, axis=0)
    own = jnp.sum(total, axis=1)
    for i in range(out_ref.shape[0]):
        out_ref[i] = own


def finish_kernel(channels, back_ref, gate_ref, energy_ref, gain_ref, out_ref):
    owners, rows, _ = back_ref.shape
    energy = jnp.sum(energy_ref[...], axis=0)
    scale = lax.rsqrt(energy / channels + EPSILON)
    values = back_ref[...].astype(F32)
    gain = gain_ref[...]
    for a in range(rows // GROUP):
        block = values[:, a * GROUP : (a + 1) * GROUP, :].reshape(owners * GROUP, LANES)
        block = (block * scale[a : a + 1, :]).T
        span = slice(a * LANES, (a + 1) * LANES)
        out_ref[span, :] = (gate_ref[span, :].astype(F32) * block * gain).astype(BF16)


def per_device(gate_in, key_in, value_in, filters, skip, gain):
    rows, channels = key_in.shape
    ctx = lax.axis_size("ctx")
    tp = lax.axis_size("tp")
    blocks = rows // LANES
    here = blocks * GROUP
    params = pltpu.CompilerParams(vmem_limit_bytes=32 * 1024 * 1024)
    packed = pl.pallas_call(
        pack_kernel,
        out_shape=jax.ShapeDtypeStruct((ctx, 2 * here, LANES), BF16),
        in_specs=[whole()] * 3,
        out_specs=whole(),
        compiler_params=params,
        name="pack",
    )(key_in, value_in, filters)
    recv = lax.all_to_all(packed, "ctx", split_axis=0, concat_axis=0, tiled=True)
    own_skip = lax.dynamic_slice(skip, (lax.axis_index("ctx") * GROUP,), (GROUP,))
    summed = pl.pallas_call(
        conv_kernel,
        out_shape=jax.ShapeDtypeStruct((ctx, here, LANES), BF16),
        in_specs=[whole(), pl.BlockSpec(memory_space=pltpu.SMEM)],
        out_specs=whole(),
        scratch_shapes=[
            pltpu.VMEM((ctx * here, LANES), F32),
            pltpu.VMEM((ctx * here, LANES), F32),
            pltpu.VMEM((ctx * here, LANES), F32),
            pltpu.VMEM((PAD + LANES, LANES), F32),
            pltpu.VMEM((8 + LANES, LANES), F32),
            pltpu.VMEM((8 + LANES, LANES), F32),
            pltpu.VMEM((LANES, 2 * LANES), F32),
            pltpu.VMEM((8 * LANES, 2 * LANES), BF16),
            pltpu.VMEM((8 * LANES, 2 * LANES), BF16),
        ],
        compiler_params=params,
        name="conv",
    )(recv, own_skip)
    back = lax.all_to_all(summed, "ctx", split_axis=0, concat_axis=0, tiled=True)
    own = pl.pallas_call(
        energy_kernel,
        out_shape=jax.ShapeDtypeStruct((tp, blocks, LANES), F32),
        in_specs=[whole()],
        out_specs=whole(),
        compiler_params=params,
        name="energy",
    )(back)
    energy = lax.all_to_all(own, "tp", split_axis=0, concat_axis=0, tiled=True)
    return pl.pallas_call(
        functools.partial(finish_kernel, channels * tp),
        out_shape=jax.ShapeDtypeStruct((rows, channels), BF16),
        in_specs=[whole()] * 4,
        out_specs=whole(),
        compiler_params=params,
        name="finish",
    )(back, gate_in, energy, gain.reshape(1, channels))


def solution(mesh):
    in_specs = (P("ctx", "tp"), P("ctx", "tp"), P("ctx", "tp"), P("ctx", "tp"), P("tp"), P("tp"))
    out_specs = P("ctx", "tp")
    return jax.shard_map(
        per_device, mesh=mesh, in_specs=in_specs, out_specs=out_specs, check_vma=False
    )
```

time: 315 us -> 83.2 us (0.26); the launches traced: 309 us -> 82.8 us
  waiting for transfers between devices: 134 us -> 13.5 us
  matrix products: 46.2 us -> 0 us
  blocking collectives: 76 us -> 38.3 us
  starting transfers between devices: 31.1 us -> 10.5 us
  Pallas kernels: 0 us -> 16.1 us
  local copies, waits for them, and re-layouts: 17.8 us -> 4.28 us
  other arithmetic: 3.36 us -> 0 us
    all_to_all x5 -> x1, waiting for transfers between devices: 134 us -> 13.5 us  [per_device(): lax.all_to_all(packed, 'ctx', split_axis=0, concat_axis=0, tiled=True)]
    dot_general x20 -> x0, matrix products: 46.2 us -> none  [the longest x18 44 us: contract(): return jnp.einsum(spec, table, data, precision=HIGHEST_PREC)]
    psum x1 -> x0, blocking collectives: 36.1 us -> none  [per_device(): energy = lax.psum(jnp.sum(summed * summed, axis=1), 'tp')]
    all_to_all x5 -> x1, starting transfers between devices: 31.1 us -> 10.5 us  [per_device(): lax.all_to_all(packed, 'ctx', split_axis=0, concat_axis=0, tiled=True)]
    pallas_call x0 -> x4, Pallas kernels: none -> 16.1 us  [the longest x1 14.2 us: per_device(): pl.pallas_call(conv_kernel, out_shape=jax.ShapeDtypeStruct((ctx, here, LA...]
    all_to_all x10 -> x0, local copies, waits for them, and re-layouts: 5.47 us -> none  [the longest x1 1.92 us: sequence_conv(): lax.all_to_all(part_re, 'ctx', split_axis=1, concat_axis=2, tiled=True)]
    sub x2 -> x0, local copies, waits for them, and re-layouts: 4.75 us -> none  [the longest x1 4.14 us: sequence_conv(): part_re * twist_cos - part_im * twist_sin]
    unnamed x10 -> x12, local copies, waits for them, and re-layouts: 0.32 us -> 4.2 us
  transfers between devices with their start and end apart: 5 -> 1, of which waited for: 5 -> 1; matrix products, arithmetic and copies ran while one was open for 5% -> 0% of each run, Pallas kernels for 0% -> 0%
where the time goes in v1:
time: 83.2 us; the launch traced here: 82.8 us
  blocking collectives  38.3 us (46%)
  Pallas kernels  16.1 us (19%)
  waiting for transfers between devices  13.5 us (16%)
  starting transfers between devices  10.5 us (13%)
  local copies, waits for them, and re-layouts  4.28 us (5%)
    all_to_all x1, blocking collectives, per_device(): energy = lax.all_to_all(own, 'tp', split_axis=0, concat_axis=0, tiled=True)  21.3 us
    all_to_all x1, blocking collectives, per_device(): lax.all_to_all(summed, 'ctx', split_axis=0, concat_axis=0, tiled=True)  16.9 us
    pallas_call x1, Pallas kernels, per_device(): pl.pallas_call(conv_kernel, out_shape=jax.ShapeDtypeStruct((ctx, here, LA...  14.2 us
    all_to_all x1, waiting for transfers between devices, per_device(): lax.all_to_all(packed, 'ctx', split_axis=0, concat_axis=0, tiled=True)  13.5 us
    all_to_all x1, starting transfers between devices, per_device(): lax.all_to_all(packed, 'ctx', split_axis=0, concat_axis=0, tiled=True)  10.5 us
    unnamed x12, local copies, waits for them, and re-layouts  4.2 us
  transfers between devices with their start and end apart: 1, of which 1 were waited for; matrix products, arithmetic and copies ran while one was open for 0% of the time, Pallas kernels for 0%

profile of v1, /device:TPU:1, one launch (start us, length us, event | category | flops | bytes accessed | tf_op | source)
XLA Modules:
  0.0 82.8 jit_solution(2639706069459170278)
XLA Ops:
  0.0 0.0 copy-start
  0.0 0.9 %copy-done = bf16[512,256]{1,0:T(8,128)(2,1)S(1)} copy-done((bf16[512,256]{1,0:T(8,128)(2,1)S(1)}, bf16[512,256]{1,0:T(8,128)(2,1)}, u32[]{:S(2)}) %copy-start) | copy-done | bytes 262168
  1.0 0.0 copy-start.1
  1.0 0.9 %copy-done.1 = bf16[512,256]{1,0:T(8,128)(2,1)S(1)} copy-done((bf16[512,256]{1,0:T(8,128)(2,1)S(1)}, bf16[512,256]{1,0:T(8,128)(2,1)}, u32[]{:S(2)}) %copy-start.1) | copy-done | bytes 262168
  1.9 0.0 copy-start.2
  1.9 0.9 %copy-done.2 = bf16[512,256]{1,0:T(8,128)(2,1)S(1)} copy-done((bf16[512,256]{1,0:T(8,128)(2,1)S(1)}, bf16[512,256]{1,0:T(8,128)(2,1)}, u32[]{:S(2)}) %copy-start.2) | copy-done | bytes 262168
  2.9 1.0 %pack.1 = bf16[32,64,128]{2,1,0:T(8,128)(2,1)} custom-call(bf16[512,256]{1,0:T(8,128)(2,1)S(1)} %copy-done, bf16[512,256]{1,0:T(8,128)(2,1)S(1)} %copy-done.1, bf16[512,256]{1,0:T(8,128)(2,1)S(1)} %copy-done.2), custom_call_target="tpu_custom_call" | custom-call | tf_op jit(solution)/shard_map/pack/pallas_call | solution.py:115
  3.9 10.5 %all-to-all-start = ((bf16[32,64,128]{2,1,0:T(8,128)(2,1)}), bf16[32,64,128]{2,1,0:T(8,128)(2,1)S(1)}, u32[]{:S(2)}, u32[]{:S(2)}) async-start(bf16[32,64,128]{2,1,0:T(8,128)(2,1)} %pack.1), calls=%async_computation | async-start | bytes 1048576 | tf_op jit(solution)/shard_map/all_to_all | solution.py:123
  14.4 0.0 copy-start.5
  14.4 0.7 copy-done.5
  15.0 0.1 dynamic_slice.3.skip_ref
  15.1 13.5 %all-to-all-done.recv_ref = bf16[32,64,128]{2,1,0:T(8,128)(2,1)S(1)} async-done(((bf16[32,64,128]{2,1,0:T(8,128)(2,1)}), bf16[32,64,128]{2,1,0:T(8,128)(2,1)S(1)}, u32[]{:S(2)}, u32[]{:S(2)}) %all-to-all-start) | async-done | bytes 524320 | tf_op jit(solution)/shard_map/all_to_all | solution.py:123
  28.7 14.2 %conv.1 = bf16[32,32,128]{2,1,0:T(8,128)(2,1)S(1)} custom-call(bf16[32,64,128]{2,1,0:T(8,128)(2,1)S(1)} %all-to-all-done.recv_ref, f32[8]{0:T(128)S(1)} %dynamic_slice.3.skip_ref), custom_call_target="tpu_custom_call" | custom-call | tf_op jit(solution)/shard_map/conv/pallas_call | solution.py:125
  42.8 16.9 %all_to_all.15.back_ref = bf16[32,32,128]{2,1,0:T(8,128)(2,1)S(1)} all-to-all(bf16[32,32,128]{2,1,0:T(8,128)(2,1)S(1)} %conv.1), channel_id=1, replica_groups=mesh['ctx'=32,'tp'=16] {'ctx'}, dimensions={0} | all-to-all | bytes 524288 | tf_op jit(solution)/shard_map/all_to_all | solution.py:144
  59.8 0.0 copy-start.3
  59.8 21.3 %all_to_all.16.energy_ref = f32[16,4,128]{2,1,0:T(4,128)S(1)} all-to-all(f32[16,4,128]{2,1,0:T(4,128)S(1)} %energy.1), channel_id=1, replica_groups=mesh['ctx'=32,'tp'=16] {'tp'}, dimensions={0} | all-to-all | bytes 65536 | tf_op jit(solution)/shard_map/all_to_all | solution.py:153
  81.2 0.0 copy-start.4
  81.2 0.0 copy-done.3
  81.2 0.7 copy-done.4
  81.8 0.9 %finish.1 = bf16[512,256]{1,0:T(8,128)(2,1)} custom-call(bf16[32,32,128]{2,1,0:T(8,128)(2,1)S(1)} %all_to_all.15.back_ref, bf16[512,256]{1,0:T(8,128)(2,1)S(1)} %copy-done.3, f32[16,4,128]{2,1,0:T(4,128)S(1)} %all_to_all.16.energy_ref, f32[1,256]{1,0:T(1,128)S(1)} %bitcast.1), custom_call_target="tpu_custom_call" | custom-call | tf_op jit(solution)/shard_map/finish/pallas_call | solution.py:154
  (1 shorter events, 0.0 us)
Async XLA Ops:
  0.0 0.9 %copy-start = (bf16[512,256]{1,0:T(8,128)(2,1)S(1)}, bf16[512,256]{1,0:T(8,128)(2,1)}, u32[]{:S(2)}) copy-start(bf16[512,256]{1,0:T(8,128)(2,1)} %key_ref.1) | copy-start | bytes 786436
  1.0 0.9 %copy-start.1 = (bf16[512,256]{1,0:T(8,128)(2,1)S(1)}, bf16[512,256]{1,0:T(8,128)(2,1)}, u32[]{:S(2)}) copy-start(bf16[512,256]{1,0:T(8,128)(2,1)} %value_ref.1) | copy-start | bytes 786436
  1.9 0.9 %copy-start.2 = (bf16[512,256]{1,0:T(8,128)(2,1)S(1)}, bf16[512,256]{1,0:T(8,128)(2,1)}, u32[]{:S(2)}) copy-start(bf16[512,256]{1,0:T(8,128)(2,1)} %taps_ref.1) | copy-start | bytes 786436
  3.9 24.8 %all-to-all-start = ((bf16[32,64,128]{2,1,0:T(8,128)(2,1)}), bf16[32,64,128]{2,1,0:T(8,128)(2,1)S(1)}, u32[]{:S(2)}, u32[]{:S(2)}) async-start(bf16[32,64,128]{2,1,0:T(8,128)(2,1)} %pack.1), calls=%async_computation | async-start | bytes 1048576 | tf_op jit(solution)/shard_map/all_to_all | solution.py:123
  14.4 0.7 copy-start.5
  59.8 21.4 %copy-start.3 = (bf16[512,256]{1,0:T(8,128)(2,1)S(1)}, bf16[512,256]{1,0:T(8,128)(2,1)}, u32[]{:S(2)}) copy-start(bf16[512,256]{1,0:T(8,128)(2,1)} %gate_ref.1) | copy-start | bytes 786436
  81.2 0.7 copy-start.4

commit v2 on v1

v2 whole, which is shorter than its diff:
```python
import functools

import jax
import jax.numpy as jnp
from jax import lax
from jax.experimental import pallas as pl
from jax.experimental.pallas import tpu as pltpu
from jax.sharding import PartitionSpec as P

EPSILON = 1e-05
LANES = 128
GROUP = 8
HOP = 32
STEP = 256
F32 = jnp.float32
BF16 = jnp.bfloat16


def whole():
    return pl.BlockSpec(memory_space=pltpu.VMEM)


def anywhere():
    return pl.BlockSpec(memory_space=pl.ANY)


def anywhere():
    return pl.BlockSpec(memory_space=pltpu.HBM)


def flip_blocks(rows):
    parts = []
    for a in range(rows.shape[0] // LANES):
        block = rows[a * LANES : (a + 1) * LANES, :].T
        parts.append(block.reshape(block.shape[0] // GROUP, GROUP, LANES))
    return jnp.concatenate(parts, axis=1)


def pack_kernel(
    place_ref, key_ref, value_ref, taps_ref, skip_ref, gain_ref, out_ref, rows_ref, key, value, taps, skip, in_sem
):
    half = out_ref.shape[1] // 2
    gain = rows_ref.at[GROUP:, :]
    loads = []
    pairs = ((taps_ref, taps), (key_ref, key), (value_ref, value), (skip_ref, skip), (gain_ref, gain))
    for i, (src, dst) in enumerate(pairs):
        load = pltpu.make_async_copy(src, dst, in_sem.at[i])
        load.start()
        loads.append(load)
    loads[0].wait()
    out_ref[:, half:, :] = flip_blocks(taps[...].astype(F32)).astype(BF16)
    loads[1].wait()
    loads[2].wait()
    mixed = key[...].astype(F32) * value[...].astype(F32)
    out_ref[:, :half, :] = flip_blocks(mixed).astype(BF16)
    loads[3].wait()
    loads[4].wait()
    for c in range(GROUP):
        rows_ref[c : c + 1, :] = jnp.full((1, LANES), skip[place_ref[0] * GROUP + c], F32)


def conv_kernel(
    recv_ref, rows_ref, out_ref, x_all, h_all, y_all, x_pad, h_pad, s_pad, acc, toe_0, toe_1, lhs_0, lhs_1
):
    owners, both, _ = recv_ref.shape
    half = both // 2
    x_all[...] = recv_ref[:, :half, :].astype(F32).reshape(owners * half, LANES)
    h_all[...] = recv_ref[:, half:, :].astype(F32).reshape(owners * half, LANES)
    x_pad[:8, :] = jnp.zeros((8, LANES), F32)
    h_pad[:8, :] = jnp.zeros((8, LANES), F32)
    s_pad[:, :8, :] = jnp.zeros((2, 8, LANES), F32)
    lane = lax.broadcasted_iota(jnp.int32, (8, LANES), 1)
    row = lax.broadcasted_iota(jnp.int32, (8, LANES), 0)
    edge = lane + row
    quarter = lax.broadcasted_iota(jnp.int32, (LANES, LANES), 1) // HOP
    toes = (toe_0, toe_1)
    sides = (lhs_0, lhs_1)

    def prepare(c):
        toe, side = toes[c % 2], sides[c % 2]
        h_pad[8:, :] = h_all[pl.ds(c, LANES, stride=GROUP), :]
        for k in range(LANES):
            now = jnp.broadcast_to(h_pad[8 + k : 9 + k, :], (8, LANES))
            before = jnp.broadcast_to(h_pad[7 + k : 8 + k, :], (8, LANES))
            tiles = []
            for v in range(0, HOP, 8):
                source = jnp.where(edge >= LANES - v, before, now)
                tiles.append(pltpu.roll(source, v, 1, stride=1, stride_axis=0))
            toe[k // 2 * HOP : (k // 2 + 1) * HOP, k % 2 * LANES : (k % 2 + 1) * LANES] = (
                jnp.concatenate(tiles, axis=0).astype(BF16)
            )
        x = x_all[pl.ds(c, LANES, stride=GROUP), :]
        x_pad[8:, :] = x
        late = [x] + [x_pad[8 - 2 * b : 8 - 2 * b + LANES, :] for b in (1, 2, 3)]
        turned = []
        for d in range(4):
            pick = late[d]
            for j in (1, 2, 3):
                pick = jnp.where(quarter == j, late[(j + d) % 4], pick)
            turned.append(pltpu.roll(pick, HOP * d, 1) if d else pick)
        for i in range(4):
            wide = turned[(-i) % 4]
            for b in (1, 2, 3):
                wide = jnp.where(quarter == b, turned[(b - i) % 4], wide)
            lower = jnp.concatenate([jnp.zeros((8, LANES), F32), wide[:-8]], axis=0)
            pair = jnp.concatenate([wide, lower], axis=1).astype(BF16)
            side[i, :, :STEP] = pair
            side[i, :, STEP:] = jnp.concatenate([jnp.zeros((16, STEP), BF16), pair[:-16]], axis=0)

    def convolve(c):
        toe, side = toes[c % 2], sides[c % 2]
        for g in range(0, 8, 2):
            live = LANES - 16 * g
            left = jnp.concatenate([side[i, :live, :] for i in range(4)], axis=0)
            part = jnp.dot(left, toe[STEP * g : STEP * (g + 2), :], preferred_element_type=F32)
            for i in range(4):
                if g == 0:
                    acc[i] = part[i * live : (i + 1) * live]
                else:
                    acc[i, 16 * g :, :] += part[i * live : (i + 1) * live]
        same, next_1, next_2 = acc[0, :, :LANES], acc[0, :, LANES:], jnp.zeros((LANES, LANES), F32)
        for i in range(1, 4):
            near = pltpu.roll(acc[i, :, :LANES], HOP * i, 1)
            far = pltpu.roll(acc[i, :, LANES:], HOP * i, 1)
            wrapped = quarter < i
            same = same + jnp.where(wrapped, 0.0, near)
            next_1 = next_1 + jnp.where(wrapped, near, far)
            next_2 = next_2 + jnp.where(wrapped, far, 0.0)
        s_pad[0, 8:, :] = next_1
        s_pad[1, 8:, :] = next_2
        x = x_all[pl.ds(c, LANES, stride=GROUP), :]
        conv = same + s_pad[0, 7 : 7 + LANES, :] + s_pad[1, 6 : 6 + LANES, :]
        y_all[pl.ds(c, LANES, stride=GROUP), :] = conv + rows_ref[c : c + 1, :] * x

    prepare(0)
    for c in range(GROUP):
        if c + 1 < GROUP:
            prepare(c + 1)
        convolve(c)
    out_ref[...] = y_all[...].reshape(out_ref.shape).astype(BF16)


def gate_kernel(back_ref, gate_ref, rows_ref, energy_ref, out_ref):
    owners, rows, _ = back_ref.shape
    blocks = rows // GROUP
    values = back_ref[...].astype(F32).reshape(owners, blocks, GROUP, LANES)
    own = jnp.sum(jnp.sum(values * values, axis=0), axis=1)
    for i in range(energy_ref.shape[0]):
        energy_ref[i] = own
    for a in range(blocks):
        block = values[:, a].reshape(owners * GROUP, LANES)
        span = slice(a * LANES, (a + 1) * LANES)
        for b in range(block.shape[0] // LANES):
            part = slice(b * LANES, (b + 1) * LANES)
            gain = rows_ref[GROUP + b : GROUP + b + 1, :]
            out_ref[span, part] = gate_ref[span, part].astype(F32) * block[part, :].T * gain


def scale_kernel(channels, gated_ref, energy_ref, out_ref, staged, sem):
    energy = jnp.sum(energy_ref[...], axis=0)
    scale = lax.rsqrt(energy / channels + EPSILON)
    stores = []
    for a in range(scale.shape[0]):
        column = jnp.broadcast_to(scale[a : a + 1, :], (LANES, LANES)).T
        span = slice(a * LANES, (a + 1) * LANES)
        for b in range(0, staged.shape[1], LANES):
            staged[span, b : b + LANES] = (gated_ref[span, b : b + LANES] * column).astype(BF16)
        store = pltpu.make_async_copy(staged.at[span, :], out_ref.at[span, :], sem.at[a])
        store.start()
        stores.append(store)
    for store in stores:
        store.wait()


def per_device(gate_in, key_in, value_in, filters, skip, gain):
    rows, channels = key_in.shape
    ctx = lax.axis_size("ctx")
    tp = lax.axis_size("tp")
    blocks = rows // LANES
    here = blocks * GROUP
    params = pltpu.CompilerParams(vmem_limit_bytes=32 * 1024 * 1024)
    packed, small = pl.pallas_call(
        pack_kernel,
        out_shape=[
            jax.ShapeDtypeStruct((ctx, 2 * here, LANES), BF16),
            jax.ShapeDtypeStruct((GROUP + channels // LANES, LANES), F32),
        ],
        in_specs=[pl.BlockSpec(memory_space=pltpu.SMEM)] + [anywhere()] * 5,
        out_specs=[whole()] * 2,
        scratch_shapes=[pltpu.VMEM((rows, channels), BF16)] * 3
        + [pltpu.SMEM((channels,), F32), pltpu.SemaphoreType.DMA((5,))],
        name="pack",
    )(lax.axis_index("ctx").reshape(1), key_in, value_in, filters, skip, gain.reshape(-1, LANES))
    recv = lax.all_to_all(packed, "ctx", split_axis=0, concat_axis=0, tiled=True)
    summed = pl.pallas_call(
        conv_kernel,
        out_shape=jax.ShapeDtypeStruct((ctx, here, LANES), BF16),
        in_specs=[whole()] * 2,
        out_specs=whole(),
        scratch_shapes=[pltpu.VMEM((ctx * here, LANES), F32)] * 3
        + [
            pltpu.VMEM((8 + LANES, LANES), F32),
            pltpu.VMEM((8 + LANES, LANES), F32),
            pltpu.VMEM((2, 8 + LANES, LANES), F32),
            pltpu.VMEM((4, LANES, STEP), F32),
            pltpu.VMEM((LANES // 2 * HOP, STEP), BF16),
            pltpu.VMEM((LANES // 2 * HOP, STEP), BF16),
            pltpu.VMEM((4, LANES, 2 * STEP), BF16),
            pltpu.VMEM((4, LANES, 2 * STEP), BF16),
        ],
        compiler_params=params,
        name="conv",
    )(recv, small)
    back = lax.all_to_all(summed, "ctx", split_axis=0, concat_axis=0, tiled=True)
    own, gated = pl.pallas_call(
        gate_kernel,
        out_shape=[
            jax.ShapeDtypeStruct((tp, blocks, LANES), F32),
            jax.ShapeDtypeStruct((rows, channels), F32),
        ],
        in_specs=[whole()] * 3,
        out_specs=[whole()] * 2,
        compiler_params=params,
        name="gate",
    )(back, gate_in, small)
    energy = lax.all_to_all(own, "tp", split_axis=0, concat_axis=0, tiled=True)
    return pl.pallas_call(
        functools.partial(scale_kernel, channels * tp),
        out_shape=jax.ShapeDtypeStruct((rows, channels), BF16),
        in_specs=[whole()] * 2,
        out_specs=anywhere(),
        scratch_shapes=[pltpu.VMEM((rows, channels), BF16), pltpu.SemaphoreType.DMA((blocks,))],
        compiler_params=params,
        name="scale",
    )(gated, energy)


def solution(mesh):
    in_specs = (P("ctx", "tp"), P("ctx", "tp"), P("ctx", "tp"), P("ctx", "tp"), P("tp"), P("tp"))
    out_specs = P("ctx", "tp")
    return jax.shard_map(
        per_device, mesh=mesh, in_specs=in_specs, out_specs=out_specs, check_vma=False
    )
```

time: 83.2 us -> 71.9 us (0.86)
  blocking collectives: 38.3 us -> 63.1 us
  waiting for transfers between devices: 13.5 us -> 0 us
  starting transfers between devices: 10.5 us -> 0 us
  Pallas kernels: 16.1 us -> 8.41 us
  local copies, waits for them, and re-layouts: 4.28 us -> 0.01 us
    all_to_all x0 -> x1, blocking collectives: none -> 24.8 us  [per_device(): lax.all_to_all(packed, 'ctx', split_axis=0, concat_axis=0, tiled=True)]
    all_to_all x1 -> x0, waiting for transfers between devices: 13.5 us -> none  [per_device(): lax.all_to_all(packed, 'ctx', split_axis=0, concat_axis=0, tiled=True)]
    all_to_all x1 -> x0, starting transfers between devices: 10.5 us -> none  [per_device(): lax.all_to_all(packed, 'ctx', split_axis=0, concat_axis=0, tiled=True)]
    pallas_call x1, Pallas kernels: 14.2 us -> 5.31 us  [per_device(): pl.pallas_call(conv_kernel, out_shape=jax.ShapeDtypeStruct((ctx, here, LA...]
    unnamed x12 -> x4, local copies, waits for them, and re-layouts: 4.2 us -> 0.01 us
    pallas_call x3, Pallas kernels: 1.97 us -> 3.09 us  [the longest x1 2.1 us: per_device(): pl.pallas_call(pack_kernel, out_shape=[jax.ShapeDtypeStruct((ctx, 2 * her...]
  transfers between devices with their start and end apart: 1 -> 0, of which waited for: 1 -> 0; matrix products, arithmetic and copies ran while one was open for 0% -> 0% of each run, Pallas kernels for 0% -> 0%
where the time goes in v2:
time: 71.9 us; the launch traced here: 71.6 us
  blocking collectives  63.1 us (88%)
  Pallas kernels  8.41 us (12%)
    all_to_all x1, blocking collectives, per_device(): lax.all_to_all(packed, 'ctx', split_axis=0, concat_axis=0, tiled=True)  24.8 us
    all_to_all x1, blocking collectives, per_device(): energy = lax.all_to_all(own, 'tp', split_axis=0, concat_axis=0, tiled=True)  21.2 us
    all_to_all x1, blocking collectives, per_device(): lax.all_to_all(summed, 'ctx', split_axis=0, concat_axis=0, tiled=True)  17.1 us
    pallas_call x1, Pallas kernels, per_device(): pl.pallas_call(conv_kernel, out_shape=jax.ShapeDtypeStruct((ctx, here, LA...  5.31 us
    pallas_call x1, Pallas kernels, per_device(): pl.pallas_call(pack_kernel, out_shape=[jax.ShapeDtypeStruct((ctx, 2 * her...  2.1 us

profile of v2, /device:TPU:1, one launch (start us, length us, event | category | flops | bytes accessed | tf_op | source)
XLA Modules:
  0.0 71.6 jit_solution(9669792315092466485)
XLA Ops:
  0.0 2.1 %pack.1 = (bf16[32,64,128]{2,1,0:T(8,128)(2,1)}, f32[10,128]{1,0:T(8,128)}) custom-call(s32[1]{0:T(128)} %bitcast.place_ref, bf16[512,256]{1,0:T(8,128)(2,1)} %key_ref.1, bf16[512,256]{1,0:T(8,128)(2,1)} %value_ref.1, bf16[512,256]{1,0:T(8,128)(2,1)} %taps_ref.1, f32[256]{0:T(256)} %skip_ref.1, f32[2,128]{1,0:T(2,128)} %bitcast.2), custom_call_target="tpu_custom_call" | custom-call | tf_op jit(solution)/shard_map/pack/pallas_call | solution.py:182
  2.1 0.0 copy-start.1
  2.1 24.8 %all_to_all.15.recv_ref = bf16[32,64,128]{2,1,0:T(8,128)(2,1)S(1)} all-to-all(bf16[32,64,128]{2,1,0:T(8,128)(2,1)} %get-tuple-element.9), channel_id=1, replica_groups=mesh['ctx'=32,'tp'=16] {'ctx'}, dimensions={0} | all-to-all | bytes 1048576 | tf_op jit(solution)/shard_map/all_to_all | solution.py:194
  26.9 0.0 copy-done.1
  26.9 5.3 %conv.1 = bf16[32,32,128]{2,1,0:T(8,128)(2,1)S(1)} custom-call(bf16[32,64,128]{2,1,0:T(8,128)(2,1)S(1)} %all_to_all.15.recv_ref, f32[10,128]{1,0:T(8,128)S(1)} %copy-done.1), custom_call_target="tpu_custom_call" | custom-call | tf_op jit(solution)/shard_map/conv/pallas_call | solution.py:195
  32.3 0.0 copy-start
  32.3 17.1 %all_to_all.16.back_ref = bf16[32,32,128]{2,1,0:T(8,128)(2,1)S(1)} all-to-all(bf16[32,32,128]{2,1,0:T(8,128)(2,1)S(1)} %conv.1), channel_id=1, replica_groups=mesh['ctx'=32,'tp'=16] {'ctx'}, dimensions={0} | all-to-all | bytes 524288 | tf_op jit(solution)/shard_map/all_to_all | solution.py:214
  49.4 0.0 copy-done
  49.4 0.1 gate.1
  49.5 21.2 %all_to_all.17.energy_ref = f32[16,4,128]{2,1,0:T(4,128)S(1)} all-to-all(f32[16,4,128]{2,1,0:T(4,128)S(1)} %get-tuple-element.12), channel_id=1, replica_groups=mesh['ctx'=32,'tp'=16] {'tp'}, dimensions={0} | all-to-all | bytes 65536 | tf_op jit(solution)/shard_map/all_to_all | solution.py:226
  70.7 0.9 %scale.1 = bf16[512,256]{1,0:T(8,128)(2,1)} custom-call(f32[512,256]{1,0:T(8,128)S(1)} %get-tuple-element.11.gated_ref, f32[16,4,128]{2,1,0:T(4,128)S(1)} %all_to_all.17.energy_ref), custom_call_target="tpu_custom_call" | custom-call | tf_op jit(solution)/shard_map/scale/pallas_call | solution.py:227
Async XLA Ops:
  2.1 24.8 %copy-start.1 = (f32[10,128]{1,0:T(8,128)S(1)}, f32[10,128]{1,0:T(8,128)}, u32[]{:S(2)}) copy-start(f32[10,128]{1,0:T(8,128)} %get-tuple-element.10.rows_ref) | copy-start | bytes 15364
  32.3 17.1 %copy-start = (bf16[512,256]{1,0:T(8,128)(2,1)S(1)}, bf16[512,256]{1,0:T(8,128)(2,1)}, u32[]{:S(2)}) copy-start(bf16[512,256]{1,0:T(8,128)(2,1)} %gate_ref.1) | copy-start | bytes 786436

commit v3 on v2

--- a/solution.py
+++ b/solution.py
@@ -12,6 +12,7 @@
 GROUP = 8
 HOP = 32
 STEP = 256
+ROWS = 32
 F32 = jnp.float32
 BF16 = jnp.bfloat16
 
@@ -60,7 +61,7 @@
 
 
 def conv_kernel(
-    recv_ref, rows_ref, out_ref, x_all, h_all, y_all, x_pad, h_pad, s_pad, acc, toe_0, toe_1, lhs_0, lhs_1
+    recv_ref, rows_ref, out_ref, x_all, h_all, y_all, x_pad, h_pad, s_pad, toe_0, toe_1, side_0, side_1
 ):
     owners, both, _ = recv_ref.shape
     half = both // 2
@@ -69,17 +70,22 @@
     x_pad[:8, :] = jnp.zeros((8, LANES), F32)
     h_pad[:8, :] = jnp.zeros((8, LANES), F32)
     s_pad[:, :8, :] = jnp.zeros((2, 8, LANES), F32)
+    toes = (toe_0, toe_1)
+    sides = (side_0, side_1)
+    for side in sides:
+        side[:, :16, :] = jnp.zeros((4, 16, STEP), BF16)
     lane = lax.broadcasted_iota(jnp.int32, (8, LANES), 1)
     row = lax.broadcasted_iota(jnp.int32, (8, LANES), 0)
     edge = lane + row
-    quarter = lax.broadcasted_iota(jnp.int32, (LANES, LANES), 1) // HOP
-    toes = (toe_0, toe_1)
-    sides = (lhs_0, lhs_1)
-
-    def prepare(c):
-        toe, side = toes[c % 2], sides[c % 2]
+    quarter = lax.broadcasted_iota(jnp.int32, (ROWS, LANES), 1) // HOP
+
+    def fetch(c):
         h_pad[8:, :] = h_all[pl.ds(c, LANES, stride=GROUP), :]
-        for k in range(LANES):
+        x_pad[8:, :] = x_all[pl.ds(c, LANES, stride=GROUP), :]
+
+    def build_toe(c, s):
+        toe = toes[c % 2]
+        for k in range(ROWS * s, ROWS * (s + 1)):
             now = jnp.broadcast_to(h_pad[8 + k : 9 + k, :], (8, LANES))
             before = jnp.broadcast_to(h_pad[7 + k : 8 + k, :], (8, LANES))
             tiles = []
@@ -89,54 +95,75 @@
             toe[k // 2 * HOP : (k // 2 + 1) * HOP, k % 2 * LANES : (k % 2 + 1) * LANES] = (
                 jnp.concatenate(tiles, axis=0).astype(BF16)
             )
-        x = x_all[pl.ds(c, LANES, stride=GROUP), :]
-        x_pad[8:, :] = x
-        late = [x] + [x_pad[8 - 2 * b : 8 - 2 * b + LANES, :] for b in (1, 2, 3)]
+
+    def build_side(c, s, above):
+        side = sides[c % 2]
+        low = ROWS * s
+        late = [x_pad[8 - 2 * b + low : 8 - 2 * b + low + ROWS, :] for b in range(4)]
         turned = []
         for d in range(4):
             pick = late[d]
             for j in (1, 2, 3):
                 pick = jnp.where(quarter == j, late[(j + d) % 4], pick)
             turned.append(pltpu.roll(pick, HOP * d, 1) if d else pick)
-        for i in range(4):
-            wide = turned[(-i) % 4]
+        last = []
+        for j in range(4):
+            wide = turned[(-j) % 4]
             for b in (1, 2, 3):
-                wide = jnp.where(quarter == b, turned[(b - i) % 4], wide)
-            lower = jnp.concatenate([jnp.zeros((8, LANES), F32), wide[:-8]], axis=0)
-            pair = jnp.concatenate([wide, lower], axis=1).astype(BF16)
-            side[i, :, :STEP] = pair
-            side[i, :, STEP:] = jnp.concatenate([jnp.zeros((16, STEP), BF16), pair[:-16]], axis=0)
-
-    def convolve(c):
+                wide = jnp.where(quarter == b, turned[(b - j) % 4], wide)
+            lower = jnp.concatenate([above[j], wide[:-8]], axis=0)
+            side[j, 16 + low : 16 + low + ROWS, :] = jnp.concatenate([wide, lower], axis=1).astype(BF16)
+            last.append(wide[-8:])
+        return last
+
+    def product(c, s):
         toe, side = toes[c % 2], sides[c % 2]
-        for g in range(0, 8, 2):
-            live = LANES - 16 * g
-            left = jnp.concatenate([side[i, :live, :] for i in range(4)], axis=0)
-            part = jnp.dot(left, toe[STEP * g : STEP * (g + 2), :], preferred_element_type=F32)
-            for i in range(4):
-                if g == 0:
-                    acc[i] = part[i * live : (i + 1) * live]
-                else:
-                    acc[i, 16 * g :, :] += part[i * live : (i + 1) * live]
-        same, next_1, next_2 = acc[0, :, :LANES], acc[0, :, LANES:], jnp.zeros((LANES, LANES), F32)
-        for i in range(1, 4):
-            near = pltpu.roll(acc[i, :, :LANES], HOP * i, 1)
-            far = pltpu.roll(acc[i, :, LANES:], HOP * i, 1)
-            wrapped = quarter < i
+        count = 2 * s + 2
+        left = []
+        for j in range(4):
+            starts = [16 + ROWS * s - 16 * g for g in range(count)]
+            left.append(jnp.concatenate([side[j, i : i + ROWS, :] for i in starts], axis=1))
+        return jnp.dot(
+            jnp.concatenate(left, axis=0), toe[: STEP * count, :], preferred_element_type=F32
+        )
+
+    def overlap_add(c, s, part):
+        low = ROWS * s
+        same, next_1 = part[:ROWS, :LANES], part[:ROWS, LANES:]
+        next_2 = jnp.zeros((ROWS, LANES), F32)
+        for j in range(1, 4):
+            near = pltpu.roll(part[ROWS * j : ROWS * (j + 1), :LANES], HOP * j, 1)
+            far = pltpu.roll(part[ROWS * j : ROWS * (j + 1), LANES:], HOP * j, 1)
+            wrapped = quarter < j
             same = same + jnp.where(wrapped, 0.0, near)
             next_1 = next_1 + jnp.where(wrapped, near, far)
             next_2 = next_2 + jnp.where(wrapped, far, 0.0)
-        s_pad[0, 8:, :] = next_1
-        s_pad[1, 8:, :] = next_2
-        x = x_all[pl.ds(c, LANES, stride=GROUP), :]
-        conv = same + s_pad[0, 7 : 7 + LANES, :] + s_pad[1, 6 : 6 + LANES, :]
-        y_all[pl.ds(c, LANES, stride=GROUP), :] = conv + rows_ref[c : c + 1, :] * x
-
-    prepare(0)
+        s_pad[0, 8 + low : 8 + low + ROWS, :] = next_1
+        s_pad[1, 8 + low : 8 + low + ROWS, :] = next_2
+        conv = same + s_pad[0, 7 + low : 7 + low + ROWS, :] + s_pad[1, 6 + low : 6 + low + ROWS, :]
+        own = pl.ds(GROUP * low + c, ROWS, stride=GROUP)
+        y_all[own, :] = conv + rows_ref[c : c + 1, :] * x_all[own, :]
+
+    steps = LANES // ROWS
+    nothing = [jnp.zeros((8, LANES), F32)] * 4
+    fetch(0)
+    above = nothing
+    for s in range(steps):
+        above = build_side(0, s, above)
+        build_toe(0, s)
+    pending = None
     for c in range(GROUP):
         if c + 1 < GROUP:
-            prepare(c + 1)
-        convolve(c)
+            fetch(c + 1)
+        above = nothing
+        for s in range(steps):
+            if c + 1 < GROUP:
+                above = build_side(c + 1, s, above)
+                build_toe(c + 1, s)
+            if pending is not None:
+                overlap_add(*pending)
+            pending = (c, s, product(c, s))
+    overlap_add(*pending)
     out_ref[...] = y_all[...].reshape(out_ref.shape).astype(BF16)
 
 
@@ -189,8 +216,13 @@
         out_specs=[whole()] * 2,
         scratch_shapes=[pltpu.VMEM((rows, channels), BF16)] * 3
         + [pltpu.SMEM((channels,), F32), pltpu.SemaphoreType.DMA((5,))],
+        compiler_params=params,
         name="pack",
-    )(lax.axis_index("ctx").reshape(1), key_in, value_in, filters, skip, gain.reshape(-1, LANES))
+    )(
+        lax.axis_index("ctx").reshape(1),
+        *(pltpu.with_memory_space_constraint(v, pltpu.HBM) for v in (key_in, value_in, filters, skip)),
+        pltpu.with_memory_space_constraint(gain.reshape(-1, LANES), pltpu.HBM),
+    )
     recv = lax.all_to_all(packed, "ctx", split_axis=0, concat_axis=0, tiled=True)
     summed = pl.pallas_call(
         conv_kernel,
@@ -202,11 +234,10 @@
             pltpu.VMEM((8 + LANES, LANES), F32),
             pltpu.VMEM((8 + LANES, LANES), F32),
             pltpu.VMEM((2, 8 + LANES, LANES), F32),
-            pltpu.VMEM((4, LANES, STEP), F32),
             pltpu.VMEM((LANES // 2 * HOP, STEP), BF16),
             pltpu.VMEM((LANES // 2 * HOP, STEP), BF16),
-            pltpu.VMEM((4, LANES, 2 * STEP), BF16),
-            pltpu.VMEM((4, LANES, 2 * STEP), BF16),
+            pltpu.VMEM((4, 16 + LANES, STEP), BF16),
+            pltpu.VMEM((4, 16 + LANES, STEP), BF16),
         ],
         compiler_params=params,
         name="conv",

time: 71.9 us -> 69.9 us (0.972)
  Pallas kernels: 8.41 us -> 6.78 us
    pallas_call x1, Pallas kernels: 5.31 us -> 4.48 us  [per_device(): pl.pallas_call(conv_kernel, out_shape=jax.ShapeDtypeStruct((ctx, here, LA...]
    pallas_call x1, Pallas kernels: 2.1 us -> 1.31 us  [per_device(): pl.pallas_call(pack_kernel, out_shape=[jax.ShapeDtypeStruct((ctx, 2 * her...]
where the time goes in v3:
time: 69.9 us; the launch traced here: 69.7 us
  blocking collectives  62.9 us (90%)
  Pallas kernels  6.78 us (10%)
    all_to_all x1, blocking collectives, per_device(): lax.all_to_all(packed, 'ctx', split_axis=0, concat_axis=0, tiled=True)  24.6 us
    all_to_all x1, blocking collectives, per_device(): energy = lax.all_to_all(own, 'tp', split_axis=0, concat_axis=0, tiled=True)  21.2 us
    all_to_all x1, blocking collectives, per_device(): lax.all_to_all(summed, 'ctx', split_axis=0, concat_axis=0, tiled=True)  17.1 us
    pallas_call x1, Pallas kernels, per_device(): pl.pallas_call(conv_kernel, out_shape=jax.ShapeDtypeStruct((ctx, here, LA...  4.48 us

profile of v3, /device:TPU:1, one launch (start us, length us, event | category | flops | bytes accessed | tf_op | source)
XLA Modules:
  0.0 69.7 jit_solution(9693397790030411989)
XLA Ops:
  0.0 1.3 %pack.1 = (bf16[32,64,128]{2,1,0:T(8,128)(2,1)S(1)}, f32[10,128]{1,0:T(8,128)S(1)}) custom-call(s32[1]{0:T(128)} %bitcast.place_ref, bf16[512,256]{1,0:T(8,128)(2,1)} %key_ref.1, bf16[512,256]{1,0:T(8,128)(2,1)} %value_ref.1, bf16[512,256]{1,0:T(8,128)(2,1)} %taps_ref.1, f32[256]{0:T(256)} %skip_ref.1, f32[2,128]{1,0:T(2,128)} %bitcast.2), custom_call_target="tpu_custom_call" | custom-call | tf_op jit(solution)/shard_map/pack/pallas_call | solution.py:209
  1.3 24.6 %all_to_all.15.recv_ref = bf16[32,64,128]{2,1,0:T(8,128)(2,1)S(1)} all-to-all(bf16[32,64,128]{2,1,0:T(8,128)(2,1)S(1)} %get-tuple-element.9), channel_id=1, replica_groups=mesh['ctx'=32,'tp'=16] {'ctx'}, dimensions={0} | all-to-all | bytes 1048576 | tf_op jit(solution)/shard_map/all_to_all | solution.py:226
  25.9 4.5 %conv.1 = bf16[32,32,128]{2,1,0:T(8,128)(2,1)S(1)} custom-call(bf16[32,64,128]{2,1,0:T(8,128)(2,1)S(1)} %all_to_all.15.recv_ref, f32[10,128]{1,0:T(8,128)S(1)} %get-tuple-element.10.rows_ref), custom_call_target="tpu_custom_call" | custom-call | tf_op jit(solution)/shard_map/conv/pallas_call | solution.py:227
  30.4 0.0 copy-start
  30.4 17.1 %all_to_all.16.back_ref = bf16[32,32,128]{2,1,0:T(8,128)(2,1)S(1)} all-to-all(bf16[32,32,128]{2,1,0:T(8,128)(2,1)S(1)} %conv.1), channel_id=1, replica_groups=mesh['ctx'=32,'tp'=16] {'ctx'}, dimensions={0} | all-to-all | bytes 524288 | tf_op jit(solution)/shard_map/all_to_all | solution.py:245
  47.5 0.0 copy-done
  47.5 0.1 gate.1
  47.7 21.2 %all_to_all.17.energy_ref = f32[16,4,128]{2,1,0:T(4,128)S(1)} all-to-all(f32[16,4,128]{2,1,0:T(4,128)S(1)} %get-tuple-element.12), channel_id=1, replica_groups=mesh['ctx'=32,'tp'=16] {'tp'}, dimensions={0} | all-to-all | bytes 65536 | tf_op jit(solution)/shard_map/all_to_all | solution.py:257
  68.8 0.9 %scale.1 = bf16[512,256]{1,0:T(8,128)(2,1)} custom-call(f32[512,256]{1,0:T(8,128)S(1)} %get-tuple-element.11.gated_ref, f32[16,4,128]{2,1,0:T(4,128)S(1)} %all_to_all.17.energy_ref), custom_call_target="tpu_custom_call" | custom-call | tf_op jit(solution)/shard_map/scale/pallas_call | solution.py:258
Async XLA Ops:
  30.4 17.1 %copy-start = (bf16[512,256]{1,0:T(8,128)(2,1)S(1)}, bf16[512,256]{1,0:T(8,128)(2,1)}, u32[]{:S(2)}) copy-start(bf16[512,256]{1,0:T(8,128)(2,1)} %gate_ref.1) | copy-start | bytes 786436

commit v4 on v3

--- a/solution.py
+++ b/solution.py
@@ -61,7 +61,7 @@
 
 
 def conv_kernel(
-    recv_ref, rows_ref, out_ref, x_all, h_all, y_all, x_pad, h_pad, s_pad, toe_0, toe_1, side_0, side_1
+    recv_ref, rows_ref, out_ref, x_all, h_all, y_all, x_pad, h_pad, s_pad, far_pad, toe_0, toe_1, side_0, side_1
 ):
     owners, both, _ = recv_ref.shape
     half = both // 2
@@ -69,7 +69,8 @@
     h_all[...] = recv_ref[:, half:, :].astype(F32).reshape(owners * half, LANES)
     x_pad[:8, :] = jnp.zeros((8, LANES), F32)
     h_pad[:8, :] = jnp.zeros((8, LANES), F32)
-    s_pad[:, :8, :] = jnp.zeros((2, 8, LANES), F32)
+    s_pad[:8, :] = jnp.zeros((8, LANES), F32)
+    far_pad[:, :8, :] = jnp.zeros((4, 8, LANES), F32)
     toes = (toe_0, toe_1)
     sides = (side_0, side_1)
     for side in sides:
@@ -129,20 +130,22 @@
 
     def overlap_add(c, s, part):
         low = ROWS * s
-        same, next_1 = part[:ROWS, :LANES], part[:ROWS, LANES:]
-        next_2 = jnp.zeros((ROWS, LANES), F32)
-        for j in range(1, 4):
-            near = pltpu.roll(part[ROWS * j : ROWS * (j + 1), :LANES], HOP * j, 1)
-            far = pltpu.roll(part[ROWS * j : ROWS * (j + 1), LANES:], HOP * j, 1)
+        late = slice(7 + low, 7 + low + ROWS)
+        same, carried = None, jnp.zeros((ROWS, LANES), F32)
+        for j in range(4):
+            span = slice(ROWS * j, ROWS * (j + 1))
+            far_pad[j, 8 + low : 8 + low + ROWS, :] = part[span, LANES:]
+            total = part[span, :LANES] + far_pad[j, late, :]
+            if j == 0:
+                same = total
+                continue
+            total = pltpu.roll(total, HOP * j, 1)
             wrapped = quarter < j
-            same = same + jnp.where(wrapped, 0.0, near)
-            next_1 = next_1 + jnp.where(wrapped, near, far)
-            next_2 = next_2 + jnp.where(wrapped, far, 0.0)
-        s_pad[0, 8 + low : 8 + low + ROWS, :] = next_1
-        s_pad[1, 8 + low : 8 + low + ROWS, :] = next_2
-        conv = same + s_pad[0, 7 + low : 7 + low + ROWS, :] + s_pad[1, 6 + low : 6 + low + ROWS, :]
+            same = same + jnp.where(wrapped, 0.0, total)
+            carried = carried + jnp.where(wrapped, total, 0.0)
+        s_pad[8 + low : 8 + low + ROWS, :] = carried
         own = pl.ds(GROUP * low + c, ROWS, stride=GROUP)
-        y_all[own, :] = conv + rows_ref[c : c + 1, :] * x_all[own, :]
+        y_all[own, :] = same + s_pad[late, :] + rows_ref[c : c + 1, :] * x_all[own, :]
 
     steps = LANES // ROWS
     nothing = [jnp.zeros((8, LANES), F32)] * 4
@@ -233,7 +236,8 @@
         + [
             pltpu.VMEM((8 + LANES, LANES), F32),
             pltpu.VMEM((8 + LANES, LANES), F32),
-            pltpu.VMEM((2, 8 + LANES, LANES), F32),
+            pltpu.VMEM((8 + LANES, LANES), F32),
+            pltpu.VMEM((4, 8 + LANES, LANES), F32),
             pltpu.VMEM((LANES // 2 * HOP, STEP), BF16),
             pltpu.VMEM((LANES // 2 * HOP, STEP), BF16),
             pltpu.VMEM((4, 16 + LANES, STEP), BF16),

time: 69.9 us -> 69.7 us (level)
  no operation moved by 1% of the time
where the time goes in v4:
time: 69.7 us; the launch traced here: 69.5 us
  blocking collectives  62.9 us (90%)
  Pallas kernels  6.53 us (9%)
    all_to_all x1, blocking collectives, per_device(): lax.all_to_all(packed, 'ctx', split_axis=0, concat_axis=0, tiled=True)  24.6 us
    all_to_all x1, blocking collectives, per_device(): energy = lax.all_to_all(own, 'tp', split_axis=0, concat_axis=0, tiled=True)  21.2 us
    all_to_all x1, blocking collectives, per_device(): lax.all_to_all(summed, 'ctx', split_axis=0, concat_axis=0, tiled=True)  17.1 us
    pallas_call x1, Pallas kernels, per_device(): pl.pallas_call(conv_kernel, out_shape=jax.ShapeDtypeStruct((ctx, here, LA...  4.23 us

profile of v4, /device:TPU:1, one launch (start us, length us, event | category | flops | bytes accessed | tf_op | source)
XLA Modules:
  0.0 69.5 jit_solution(4669465128626732854)
XLA Ops:
  0.0 1.3 %pack.1 = (bf16[32,64,128]{2,1,0:T(8,128)(2,1)S(1)}, f32[10,128]{1,0:T(8,128)S(1)}) custom-call(s32[1]{0:T(128)} %bitcast.place_ref, bf16[512,256]{1,0:T(8,128)(2,1)} %key_ref.1, bf16[512,256]{1,0:T(8,128)(2,1)} %value_ref.1, bf16[512,256]{1,0:T(8,128)(2,1)} %taps_ref.1, f32[256]{0:T(256)} %skip_ref.1, f32[2,128]{1,0:T(2,128)} %bitcast.2), custom_call_target="tpu_custom_call" | custom-call | tf_op jit(solution)/shard_map/pack/pallas_call | solution.py:212
  1.3 24.6 %all_to_all.15.recv_ref = bf16[32,64,128]{2,1,0:T(8,128)(2,1)S(1)} all-to-all(bf16[32,64,128]{2,1,0:T(8,128)(2,1)S(1)} %get-tuple-element.9), channel_id=1, replica_groups=mesh['ctx'=32,'tp'=16] {'ctx'}, dimensions={0} | all-to-all | bytes 1048576 | tf_op jit(solution)/shard_map/all_to_all | solution.py:229
  25.9 4.2 %conv.1 = bf16[32,32,128]{2,1,0:T(8,128)(2,1)S(1)} custom-call(bf16[32,64,128]{2,1,0:T(8,128)(2,1)S(1)} %all_to_all.15.recv_ref, f32[10,128]{1,0:T(8,128)S(1)} %get-tuple-element.10.rows_ref), custom_call_target="tpu_custom_call" | custom-call | tf_op jit(solution)/shard_map/conv/pallas_call | solution.py:230
  30.2 0.0 copy-start
  30.2 17.1 %all_to_all.16.back_ref = bf16[32,32,128]{2,1,0:T(8,128)(2,1)S(1)} all-to-all(bf16[32,32,128]{2,1,0:T(8,128)(2,1)S(1)} %conv.1), channel_id=1, replica_groups=mesh['ctx'=32,'tp'=16] {'ctx'}, dimensions={0} | all-to-all | bytes 524288 | tf_op jit(solution)/shard_map/all_to_all | solution.py:249
  47.2 0.0 copy-done
  47.3 0.1 gate.1
  47.4 21.2 %all_to_all.17.energy_ref = f32[16,4,128]{2,1,0:T(4,128)S(1)} all-to-all(f32[16,4,128]{2,1,0:T(4,128)S(1)} %get-tuple-element.12), channel_id=1, replica_groups=mesh['ctx'=32,'tp'=16] {'tp'}, dimensions={0} | all-to-all | bytes 65536 | tf_op jit(solution)/shard_map/all_to_all | solution.py:261
  68.6 0.9 %scale.1 = bf16[512,256]{1,0:T(8,128)(2,1)} custom-call(f32[512,256]{1,0:T(8,128)S(1)} %get-tuple-element.11.gated_ref, f32[16,4,128]{2,1,0:T(4,128)S(1)} %all_to_all.17.energy_ref), custom_call_target="tpu_custom_call" | custom-call | tf_op jit(solution)/shard_map/scale/pallas_call | solution.py:262
Async XLA Ops:
  30.2 17.1 %copy-start = (bf16[512,256]{1,0:T(8,128)(2,1)S(1)}, bf16[512,256]{1,0:T(8,128)(2,1)}, u32[]{:S(2)}) copy-start(bf16[512,256]{1,0:T(8,128)(2,1)} %gate_ref.1) | copy-start | bytes 786436

commit v5 on v4

--- a/solution.py
+++ b/solution.py
@@ -13,6 +13,8 @@
 HOP = 32
 STEP = 256
 ROWS = 32
+SEND_ORDER = [8 * x + (2 * x + y) % 8 for y in range(8) for x in range(4)]
+RETURN_ORDER = [8 * x + y for y in (0, 4, 1, 5, 2, 6, 3, 7) for x in (0, 2, 1, 3)]
 F32 = jnp.float32
 BF16 = jnp.bfloat16
 
@@ -34,7 +36,8 @@
     for a in range(rows.shape[0] // LANES):
         block = rows[a * LANES : (a + 1) * LANES, :].T
         parts.append(block.reshape(block.shape[0] // GROUP, GROUP, LANES))
-    return jnp.concatenate(parts, axis=1)
+    owners = jnp.concatenate(parts, axis=1)
+    return jnp.stack([owners[d] for d in SEND_ORDER])
 
 
 def pack_kernel(
@@ -65,8 +68,9 @@
 ):
     owners, both, _ = recv_ref.shape
     half = both // 2
-    x_all[...] = recv_ref[:, :half, :].astype(F32).reshape(owners * half, LANES)
-    h_all[...] = recv_ref[:, half:, :].astype(F32).reshape(owners * half, LANES)
+    for i, d in enumerate(SEND_ORDER):
+        x_all[d * half : (d + 1) * half, :] = recv_ref[i, :half, :].astype(F32)
+        h_all[d * half : (d + 1) * half, :] = recv_ref[i, half:, :].astype(F32)
     x_pad[:8, :] = jnp.zeros((8, LANES), F32)
     h_pad[:8, :] = jnp.zeros((8, LANES), F32)
     s_pad[:8, :] = jnp.zeros((8, LANES), F32)
@@ -167,13 +171,16 @@
                 overlap_add(*pending)
             pending = (c, s, product(c, s))
     overlap_add(*pending)
-    out_ref[...] = y_all[...].reshape(out_ref.shape).astype(BF16)
+    summed = y_all[...].reshape(out_ref.shape)
+    out_ref[...] = jnp.stack([summed[d] for d in RETURN_ORDER]).astype(BF16)
 
 
 def gate_kernel(back_ref, gate_ref, rows_ref, energy_ref, out_ref):
     owners, rows, _ = back_ref.shape
     blocks = rows // GROUP
-    values = back_ref[...].astype(F32).reshape(owners, blocks, GROUP, LANES)
+    values = back_ref[...].astype(F32)
+    values = jnp.stack([values[RETURN_ORDER.index(d)] for d in range(owners)])
+    values = values.reshape(owners, blocks, GROUP, LANES)
     own = jnp.sum(jnp.sum(values * values, axis=0), axis=1)
     for i in range(energy_ref.shape[0]):
         energy_ref[i] = own
@@ -226,7 +233,9 @@
         *(pltpu.with_memory_space_constraint(v, pltpu.HBM) for v in (key_in, value_in, filters, skip)),
         pltpu.with_memory_space_constraint(gain.reshape(-1, LANES), pltpu.HBM),
     )
-    recv = lax.all_to_all(packed, "ctx", split_axis=0, concat_axis=0, tiled=True)
+    recv = lax.all_to_all(
+        packed, "ctx", split_axis=0, concat_axis=0, tiled=True, axis_index_groups=[SEND_ORDER]
+    )
     summed = pl.pallas_call(
         conv_kernel,
         out_shape=jax.ShapeDtypeStruct((ctx, here, LANES), BF16),
@@ -246,7 +255,9 @@
         compiler_params=params,
         name="conv",
     )(recv, small)
-    back = lax.all_to_all(summed, "ctx", split_axis=0, concat_axis=0, tiled=True)
+    back = lax.all_to_all(
+        summed, "ctx", split_axis=0, concat_axis=0, tiled=True, axis_index_groups=[RETURN_ORDER]
+    )
     own, gated = pl.pallas_call(
         gate_kernel,
         out_shape=[

time: 69.7 us -> 68.7 us (0.986)
  blocking collectives: 62.9 us -> 61.8 us
    all_to_all x2, blocking collectives: 41.7 us -> 40.6 us  [the longest x1 25.9 us: per_device(): lax.all_to_all(packed, 'ctx', split_axis=0, concat_axis=0, tiled=True, ax...]
where the time goes in v5:
time: 68.7 us; the launch traced here: 68.3 us
  blocking collectives  61.8 us (90%)
  Pallas kernels  6.5 us (9%)
    all_to_all x1, blocking collectives, per_device(): lax.all_to_all(packed, 'ctx', split_axis=0, concat_axis=0, tiled=True, ax...  25.9 us
    all_to_all x1, blocking collectives, per_device(): energy = lax.all_to_all(own, 'tp', split_axis=0, concat_axis=0, tiled=True)  21.2 us
    all_to_all x1, blocking collectives, per_device(): lax.all_to_all(summed, 'ctx', split_axis=0, concat_axis=0, tiled=True, ax...  14.7 us
    pallas_call x1, Pallas kernels, per_device(): pl.pallas_call(conv_kernel, out_shape=jax.ShapeDtypeStruct((ctx, here, LA...  4.2 us

profile of v5, /device:TPU:1, one launch (start us, length us, event | category | flops | bytes accessed | tf_op | source)
XLA Modules:
  0.0 68.3 jit_solution(16421294797738834350)
XLA Ops:
  0.0 1.3 %pack.1 = (bf16[32,64,128]{2,1,0:T(8,128)(2,1)S(1)}, f32[10,128]{1,0:T(8,128)S(1)}) custom-call(s32[1]{0:T(128)} %bitcast.place_ref, bf16[512,256]{1,0:T(8,128)(2,1)} %key_ref.1, bf16[512,256]{1,0:T(8,128)(2,1)} %value_ref.1, bf16[512,256]{1,0:T(8,128)(2,1)} %taps_ref.1, f32[256]{0:T(256)} %skip_ref.1, f32[2,128]{1,0:T(2,128)} %bitcast.2), custom_call_target="tpu_custom_call" | custom-call | tf_op jit(solution)/shard_map/pack/pallas_call | solution.py:219
  1.3 25.9 %all_to_all.15.recv_ref = bf16[32,64,128]{2,1,0:T(8,128)(2,1)S(1)} all-to-all(bf16[32,64,128]{2,1,0:T(8,128)(2,1)S(1)} %get-tuple-element.9), channel_id=1, replica_groups={{0,160,320,480,16,176,336,496,32,192,352,384,48,208,368,400,64,224,256,..., dimensions={0} | all-to-all | bytes 1048576 | tf_op jit(solution)/shard_map/all_to_all | solution.py:236
  27.2 4.2 %conv.1 = bf16[32,32,128]{2,1,0:T(8,128)(2,1)S(1)} custom-call(bf16[32,64,128]{2,1,0:T(8,128)(2,1)S(1)} %all_to_all.15.recv_ref, f32[10,128]{1,0:T(8,128)S(1)} %get-tuple-element.10.rows_ref), custom_call_target="tpu_custom_call" | custom-call | tf_op jit(solution)/shard_map/conv/pallas_call | solution.py:239
  31.4 0.0 copy-start
  31.4 14.7 %all_to_all.16.back_ref = bf16[32,32,128]{2,1,0:T(8,128)(2,1)S(1)} all-to-all(bf16[32,32,128]{2,1,0:T(8,128)(2,1)S(1)} %conv.1), channel_id=1, replica_groups={{0,256,128,384,64,320,192,448,16,272,144,400,80,336,208,464,32,288,160,..., dimensions={0} | all-to-all | bytes 524288 | tf_op jit(solution)/shard_map/all_to_all | solution.py:258
  46.1 0.0 copy-done
  46.1 0.1 gate.1
  46.3 21.2 %all_to_all.17.energy_ref = f32[16,4,128]{2,1,0:T(4,128)S(1)} all-to-all(f32[16,4,128]{2,1,0:T(4,128)S(1)} %get-tuple-element.12), channel_id=1, replica_groups=mesh['ctx'=32,'tp'=16] {'tp'}, dimensions={0} | all-to-all | bytes 65536 | tf_op jit(solution)/shard_map/all_to_all | solution.py:272
  67.5 0.9 %scale.1 = bf16[512,256]{1,0:T(8,128)(2,1)} custom-call(f32[512,256]{1,0:T(8,128)S(1)} %get-tuple-element.11.gated_ref, f32[16,4,128]{2,1,0:T(4,128)S(1)} %all_to_all.17.energy_ref), custom_call_target="tpu_custom_call" | custom-call | tf_op jit(solution)/shard_map/scale/pallas_call | solution.py:273
Async XLA Ops:
  31.4 14.7 %copy-start = (bf16[512,256]{1,0:T(8,128)(2,1)S(1)}, bf16[512,256]{1,0:T(8,128)(2,1)}, u32[]{:S(2)}) copy-start(bf16[512,256]{1,0:T(8,128)(2,1)} %gate_ref.1) | copy-start | bytes 786436

commit v6 on v5

--- a/solution.py
+++ b/solution.py
@@ -14,7 +14,7 @@
 STEP = 256
 ROWS = 32
 SEND_ORDER = [8 * x + (2 * x + y) % 8 for y in range(8) for x in range(4)]
-RETURN_ORDER = [8 * x + y for y in (0, 4, 1, 5, 2, 6, 3, 7) for x in (0, 2, 1, 3)]
+RETURN_ORDER = [int(format(i, "05b")[::-1], 2) for i in range(32)]
 F32 = jnp.float32
 BF16 = jnp.bfloat16
 

time: 68.7 us -> 68.6 us (level)
  no operation moved by 1% of the time
where the time goes in v6:
time: 68.6 us; the launch traced here: 68.4 us
  blocking collectives  61.9 us (90%)
  Pallas kernels  6.5 us (9%)
    all_to_all x1, blocking collectives, per_device(): lax.all_to_all(packed, 'ctx', split_axis=0, concat_axis=0, tiled=True, ax...  25.9 us
    all_to_all x1, blocking collectives, per_device(): energy = lax.all_to_all(own, 'tp', split_axis=0, concat_axis=0, tiled=True)  21.3 us
    all_to_all x1, blocking collectives, per_device(): lax.all_to_all(summed, 'ctx', split_axis=0, concat_axis=0, tiled=True, ax...  14.6 us
    pallas_call x1, Pallas kernels, per_device(): pl.pallas_call(conv_kernel, out_shape=jax.ShapeDtypeStruct((ctx, here, LA...  4.2 us

profile of v6, /device:TPU:1, one launch (start us, length us, event | category | flops | bytes accessed | tf_op | source)
XLA Modules:
  0.0 68.4 jit_solution(17733546955264447732)
XLA Ops:
  0.0 1.3 %pack.1 = (bf16[32,64,128]{2,1,0:T(8,128)(2,1)S(1)}, f32[10,128]{1,0:T(8,128)S(1)}) custom-call(s32[1]{0:T(128)} %bitcast.place_ref, bf16[512,256]{1,0:T(8,128)(2,1)} %key_ref.1, bf16[512,256]{1,0:T(8,128)(2,1)} %value_ref.1, bf16[512,256]{1,0:T(8,128)(2,1)} %taps_ref.1, f32[256]{0:T(256)} %skip_ref.1, f32[2,128]{1,0:T(2,128)} %bitcast.2), custom_call_target="tpu_custom_call" | custom-call | tf_op jit(solution)/shard_map/pack/pallas_call | solution.py:219
  1.3 25.9 %all_to_all.15.recv_ref = bf16[32,64,128]{2,1,0:T(8,128)(2,1)S(1)} all-to-all(bf16[32,64,128]{2,1,0:T(8,128)(2,1)S(1)} %get-tuple-element.9), channel_id=1, replica_groups={{0,160,320,480,16,176,336,496,32,192,352,384,48,208,368,400,64,224,256,..., dimensions={0} | all-to-all | bytes 1048576 | tf_op jit(solution)/shard_map/all_to_all | solution.py:236
  27.2 4.2 %conv.1 = bf16[32,32,128]{2,1,0:T(8,128)(2,1)S(1)} custom-call(bf16[32,64,128]{2,1,0:T(8,128)(2,1)S(1)} %all_to_all.15.recv_ref, f32[10,128]{1,0:T(8,128)S(1)} %get-tuple-element.10.rows_ref), custom_call_target="tpu_custom_call" | custom-call | tf_op jit(solution)/shard_map/conv/pallas_call | solution.py:239
  31.4 0.0 copy-start
  31.4 14.6 %all_to_all.16.back_ref = bf16[32,32,128]{2,1,0:T(8,128)(2,1)S(1)} all-to-all(bf16[32,32,128]{2,1,0:T(8,128)(2,1)S(1)} %conv.1), channel_id=1, replica_groups={{0,256,128,384,64,320,192,448,32,288,160,416,96,352,224,480,16,272,144,..., dimensions={0} | all-to-all | bytes 524288 | tf_op jit(solution)/shard_map/all_to_all | solution.py:258
  46.1 0.0 copy-done
  46.1 0.1 gate.1
  46.2 21.3 %all_to_all.17.energy_ref = f32[16,4,128]{2,1,0:T(4,128)S(1)} all-to-all(f32[16,4,128]{2,1,0:T(4,128)S(1)} %get-tuple-element.12), channel_id=1, replica_groups=mesh['ctx'=32,'tp'=16] {'tp'}, dimensions={0} | all-to-all | bytes 65536 | tf_op jit(solution)/shard_map/all_to_all | solution.py:272
  67.6 0.9 %scale.1 = bf16[512,256]{1,0:T(8,128)(2,1)} custom-call(f32[512,256]{1,0:T(8,128)S(1)} %get-tuple-element.11.gated_ref, f32[16,4,128]{2,1,0:T(4,128)S(1)} %all_to_all.17.energy_ref), custom_call_target="tpu_custom_call" | custom-call | tf_op jit(solution)/shard_map/scale/pallas_call | solution.py:273
Async XLA Ops:
  31.4 14.7 %copy-start = (bf16[512,256]{1,0:T(8,128)(2,1)S(1)}, bf16[512,256]{1,0:T(8,128)(2,1)}, u32[]{:S(2)}) copy-start(bf16[512,256]{1,0:T(8,128)(2,1)} %gate_ref.1) | copy-start | bytes 786436

commit v7 on v5

--- a/solution.py
+++ b/solution.py
@@ -158,7 +158,7 @@
     for s in range(steps):
         above = build_side(0, s, above)
         build_toe(0, s)
-    pending = None
+    pending = []
     for c in range(GROUP):
         if c + 1 < GROUP:
             fetch(c + 1)
@@ -167,10 +167,11 @@
             if c + 1 < GROUP:
                 above = build_side(c + 1, s, above)
                 build_toe(c + 1, s)
-            if pending is not None:
-                overlap_add(*pending)
-            pending = (c, s, product(c, s))
-    overlap_add(*pending)
+            if len(pending) == 2:
+                overlap_add(*pending.pop(0))
+            pending.append((c, s, product(c, s)))
+    for late in pending:
+        overlap_add(*late)
     summed = y_all[...].reshape(out_ref.shape)
     out_ref[...] = jnp.stack([summed[d] for d in RETURN_ORDER]).astype(BF16)
 

time: 68.7 us -> 68.7 us (level)
  no operation moved by 1% of the time
where the time goes in v7:
time: 68.7 us; the launch traced here: 68.3 us
  blocking collectives  61.8 us (90%)
  Pallas kernels  6.5 us (9%)
    all_to_all x1, blocking collectives, per_device(): lax.all_to_all(packed, 'ctx', split_axis=0, concat_axis=0, tiled=True, ax...  25.9 us
    all_to_all x1, blocking collectives, per_device(): energy = lax.all_to_all(own, 'tp', split_axis=0, concat_axis=0, tiled=True)  21.2 us
    all_to_all x1, blocking collectives, per_device(): lax.all_to_all(summed, 'ctx', split_axis=0, concat_axis=0, tiled=True, ax...  14.7 us
    pallas_call x1, Pallas kernels, per_device(): pl.pallas_call(conv_kernel, out_shape=jax.ShapeDtypeStruct((ctx, here, LA...  4.2 us

profile of v7, /device:TPU:1, one launch (start us, length us, event | category | flops | bytes accessed | tf_op | source)
XLA Modules:
  0.0 68.3 jit_solution(6101350011720690738)
XLA Ops:
  0.0 1.3 %pack.1 = (bf16[32,64,128]{2,1,0:T(8,128)(2,1)S(1)}, f32[10,128]{1,0:T(8,128)S(1)}) custom-call(s32[1]{0:T(128)} %bitcast.place_ref, bf16[512,256]{1,0:T(8,128)(2,1)} %key_ref.1, bf16[512,256]{1,0:T(8,128)(2,1)} %value_ref.1, bf16[512,256]{1,0:T(8,128)(2,1)} %taps_ref.1, f32[256]{0:T(256)} %skip_ref.1, f32[2,128]{1,0:T(2,128)} %bitcast.2), custom_call_target="tpu_custom_call" | custom-call | tf_op jit(solution)/shard_map/pack/pallas_call | solution.py:220
  1.3 25.9 %all_to_all.15.recv_ref = bf16[32,64,128]{2,1,0:T(8,128)(2,1)S(1)} all-to-all(bf16[32,64,128]{2,1,0:T(8,128)(2,1)S(1)} %get-tuple-element.9), channel_id=1, replica_groups={{0,160,320,480,16,176,336,496,32,192,352,384,48,208,368,400,64,224,256,..., dimensions={0} | all-to-all | bytes 1048576 | tf_op jit(solution)/shard_map/all_to_all | solution.py:237
  27.2 4.2 %conv.1 = bf16[32,32,128]{2,1,0:T(8,128)(2,1)S(1)} custom-call(bf16[32,64,128]{2,1,0:T(8,128)(2,1)S(1)} %all_to_all.15.recv_ref, f32[10,128]{1,0:T(8,128)S(1)} %get-tuple-element.10.rows_ref), custom_call_target="tpu_custom_call" | custom-call | tf_op jit(solution)/shard_map/conv/pallas_call | solution.py:240
  31.4 0.0 copy-start
  31.4 14.7 %all_to_all.16.back_ref = bf16[32,32,128]{2,1,0:T(8,128)(2,1)S(1)} all-to-all(bf16[32,32,128]{2,1,0:T(8,128)(2,1)S(1)} %conv.1), channel_id=1, replica_groups={{0,256,128,384,64,320,192,448,16,272,144,400,80,336,208,464,32,288,160,..., dimensions={0} | all-to-all | bytes 524288 | tf_op jit(solution)/shard_map/all_to_all | solution.py:259
  46.1 0.0 copy-done
  46.1 0.1 gate.1
  46.3 21.2 %all_to_all.17.energy_ref = f32[16,4,128]{2,1,0:T(4,128)S(1)} all-to-all(f32[16,4,128]{2,1,0:T(4,128)S(1)} %get-tuple-element.12), channel_id=1, replica_groups=mesh['ctx'=32,'tp'=16] {'tp'}, dimensions={0} | all-to-all | bytes 65536 | tf_op jit(solution)/shard_map/all_to_all | solution.py:273
  67.5 0.9 %scale.1 = bf16[512,256]{1,0:T(8,128)(2,1)} custom-call(f32[512,256]{1,0:T(8,128)S(1)} %get-tuple-element.11.gated_ref, f32[16,4,128]{2,1,0:T(4,128)S(1)} %all_to_all.17.energy_ref), custom_call_target="tpu_custom_call" | custom-call | tf_op jit(solution)/shard_map/scale/pallas_call | solution.py:274
Async XLA Ops:
  31.4 14.7 %copy-start = (bf16[512,256]{1,0:T(8,128)(2,1)S(1)}, bf16[512,256]{1,0:T(8,128)(2,1)}, u32[]{:S(2)}) copy-start(bf16[512,256]{1,0:T(8,128)(2,1)} %gate_ref.1) | copy-start | bytes 786436
